TPU v7x, 32 devices: a whole 2x2x4 slice. The times are simulated.
32 devices in a mesh: tile: 4 (over x, core), orient: 8 (over z, y).
Axes of the slice: x: 2, y: 2, z: 4, core: 2. Of those that a mesh axis runs over, the one named last changes fastest.
Arguments:
- micrograph: float32 [2048, 512], P('tile'), may hold values from -40 to 40
- templates: float32 [8, 256, 256], P('orient', 'tile'), may hold values from -6 to 6
- defocus_values: float32 [4], replicated, may hold values from 5000 to 20000
- defocus_group: int32 [4], P('tile'), may hold values from 0 to 3, as said below
Outputs:
- best_score: float32 [2048, 512], P(('tile', 'orient'))
- second_score: float32 [2048, 512], P(('tile', 'orient'))
- mean_score: float32 [2048, 512], P(('tile', 'orient'))
- score_variance: float32 [2048, 512], P(('tile', 'orient'))
Inputs may be any that keep to these rules, and one draw needn't show every extreme that they name: `defocus_group`: every group is used by some tile.
All inputs are finite; a program needn't handle non-finite values.
Results may differ from a plain program's by a relative error of at most 0.0003.
Values sent between devices are 32-bit elements; how exact they have to be, the bound alone decides.
A program may use at most 128 MiB of HBM per device.

v0:
```python
import math

import jax
import jax.numpy as jnp
from jax import lax
from jax.sharding import PartitionSpec as P

TPL = 256


WAVELENGTH = 0.0197
AMPLITUDE = 0.07
exact_mode = lax.Precision.HIGHEST


def padded(shard, sides, width):
    for axis, dim in sides:
        size, length = (lax.axis_size(axis), shard.shape[dim])
        up = [(i, (i + 1) % size) for i in range(size - 1)]
        down = [(j, i) for i, j in up]
        last = lax.slice_in_dim(shard, length - width, length, axis=dim)
        initial = lax.slice_in_dim(shard, 0, width, axis=dim)
        before = lax.ppermute(last, axis, up)
        after = lax.ppermute(initial, axis, down)
        shard = jnp.concatenate([before, shard, after], axis=dim)
    return shard


def merged_2(shard, axis, combine):
    everything = jax.tree.map(lambda part: lax.all_gather(part, axis), shard)
    initial = jax.tree.map(lambda part: part[0], everything)

    def turn(k, so_far):
        return combine(so_far, jax.tree.map(lambda part: part[k], everything))

    return lax.fori_loop(1, lax.axis_size(axis), turn, initial)


def product(former, latter):
    return jnp.dot(former, latter, precision=exact_mode, preferred_element_type=jnp.float32)


def fourier_tables(rows_out, cols_out, period):
    row_ids = lax.broadcasted_iota(jnp.int32, (rows_out, cols_out), 0)
    col_ids = lax.broadcasted_iota(jnp.int32, (rows_out, cols_out), 1)
    angles = (row_ids * col_ids % period).astype(jnp.float32) * (2.0 * math.pi / period)
    return (jnp.cos(angles), jnp.sin(angles))


def extend(plane, margin):
    rows_ext = padded(plane, (("tile", 0),), margin)
    return jnp.pad(rows_ext, ((0, 0), (margin, margin)))


def transform(plane, cos_rows, sin_rows, cosine, sine_table):
    left_real = product(cos_rows, plane)
    left_imag = -product(sin_rows, plane)
    spec_real = product(left_real, cosine) + product(left_imag, sine_table)
    spec_imag = product(left_imag, cosine) - product(left_real, sine_table)
    return (spec_real, spec_imag)


def full_spectrum(plane, cosine, sine_table):
    return transform(plane, cosine, sine_table, cosine, sine_table)


def combine(former, latter):
    top_value = jnp.maximum(former[0], latter[0])
    second = jnp.maximum(jnp.minimum(former[0], latter[0]), jnp.maximum(former[1], latter[1]))
    return (top_value, second, former[2] + latter[2], former[3] + latter[3])


def per_device(micrograph, templates, defocus_values, defocus_group):
    tile_rows, tile_width = micrograph.shape
    margin = TPL // 2
    ext_size = tile_width + 2 * margin
    tile_count = lax.axis_size("tile")
    cosine, sine_table = fourier_tables(ext_size, ext_size, ext_size)
    pixel_count = float(tile_rows * tile_width * tile_count)
    local_sums = (jnp.sum(micrograph), jnp.sum(micrograph * micrograph))
    totals = lax.psum((local_sums[0], local_sums[1]), "tile")
    centre = totals[0] / pixel_count
    spread = jnp.sqrt(totals[1] / pixel_count - centre * centre + 1e-05)
    centre, spread = (centre, spread)
    spec_real, spec_imag = full_spectrum(
        extend((micrograph - centre) / spread, margin), cosine, sine_table
    )
    gathered = lax.all_gather(templates, "tile", axis=1, tiled=True)
    centred = gathered - jnp.mean(gathered, axis=(1, 2), keepdims=True)
    root_mean = jnp.sqrt(jnp.mean(centred * centred, axis=(1, 2), keepdims=True) + 1e-06)
    normed = centred / (root_mean * TPL)
    extent = normed.shape[1]
    positions_f = lax.iota(jnp.int32, ext_size)
    signed_freq = (
        jnp.where(positions_f < ext_size // 2, positions_f, positions_f - ext_size).astype(
            jnp.float32
        )
        / ext_size
    )
    freq_square = signed_freq[:, None] ** 2 + signed_freq[None, :] ** 2
    group_ids = lax.iota(jnp.int32, defocus_values.shape[0])
    defocus = jnp.sum(jnp.where(group_ids == defocus_group[0], defocus_values, 0.0))
    phase_shift = math.pi * WAVELENGTH * defocus * freq_square
    contrast = -(
        math.sqrt(1.0 - AMPLITUDE * AMPLITUDE) * jnp.sin(phase_shift)
        + AMPLITUDE * jnp.cos(phase_shift)
    )
    partial_real = product(cosine[:, :extent], normed[0])
    partial_imag = -product(sine_table[:, :extent], normed[0])
    template_real = product(partial_real, cosine[:extent]) + product(
        partial_imag, sine_table[:extent]
    )
    template_imag = product(partial_imag, cosine[:extent]) - product(
        partial_real, sine_table[:extent]
    )
    product_real = (spec_real * template_real + spec_imag * template_imag) * contrast
    product_imag = (spec_imag * template_real - spec_real * template_imag) * contrast
    back_real = product(product_real, cosine[:, :tile_width]) - product(
        product_imag, sine_table[:, :tile_width]
    )
    back_imag = product(product_imag, cosine[:, :tile_width]) + product(
        product_real, sine_table[:, :tile_width]
    )
    scores = (
        product(cosine[:tile_width], back_real) - product(sine_table[:tile_width], back_imag)
    ) / (ext_size * ext_size)
    entry = (scores, jnp.full_like(scores, -jnp.inf), scores, scores * scores)
    orient_count = lax.axis_size("orient")
    share_rows = tile_rows // orient_count
    merged = merged_2((entry[0], entry[1], entry[2], entry[3]), "orient", combine)
    row_start = lax.axis_index("orient") * share_rows
    own_rows = tuple((lax.dynamic_slice_in_dim(item, row_start, share_rows, 0) for item in merged))
    total_orients = normed.shape[0] * orient_count
    mean_map = own_rows[2] / total_orients
    variance = own_rows[3] / total_orients - mean_map * mean_map
    return (own_rows[0], own_rows[1], mean_map, variance)


def solution(mesh):
    placed = (P("tile", None), P("orient", "tile", None), P(), P("tile"))
    return jax.shard_map(
        per_device,
        mesh=mesh,
        in_specs=placed,
        out_specs=(
            P(("tile", "orient"), None),
            P(("tile", "orient"), None),
            P(("tile", "orient"), None),
            P(("tile", "orient"), None),
        ),
        check_vma=False,
    )
```

profile of v0, /device:TPU:1, one launch (start us, length us, event | category | flops | bytes accessed | tf_op | source)
XLA Modules:
  0.0 492.4 jit_solution(3260584313875390276)
XLA Ops:
  9.3 7.0 %all-reduce.1 = (f32[]{:T(128)}, f32[]{:T(128)}) all-reduce(f32[]{:T(128)} %get-tuple-element.242, f32[]{:T(128)} %get-tuple-element.241), channel_id=1, replica_groups=mesh['tile'=4,'orient'=8] {'tile'}, use_global_device_ids=true, to_apply=%region_3.4 | all-reduce | flops 2 | bytes 16 | tf_op jit(solution)/shard_map/psum | solution.py:81
  21.3 3.9 collective-permute-start
  25.2 2.2 collective-permute-start.1
  27.3 9.8 %fusion.7 = f32[768,768]{1,0:T(8,128)} fusion(), kind=kLoop, calls=%fused_computation.19 | loop fusion | flops 5308416 | bytes 2359296 | tf_op jit(solution)/shard_map/cos | solution.py:47
  37.1 8.9 %fusion.6 = f32[768,768]{1,0:T(8,128)S(1)} fusion(), kind=kLoop, calls=%fused_computation.18 | loop fusion | flops 5308416 | bytes 2359296 | tf_op jit(solution)/shard_map/sin | solution.py:47
  46.0 6.3 %all_gather.18 = f32[1,256,256]{2,1,0:T(8,128)S(1)} all-gather(f32[1,64,256]{2,1,0:T(8,128)S(1)} %copy-done.4), channel_id=1, replica_groups=mesh['tile'=4,'orient'=8] {'tile'}, dimensions={1}, use_global_device_ids=true | all-gather | bytes 327680 | tf_op jit(solution)/shard_map/all_gather | solution.py:88
  56.9 3.3 fusion.67
  61.1 4.6 fusion.65
  65.7 3.6 convolution_add_fusion
  71.3 4.0 convolution_subtract_fusion
  75.3 16.3 %fusion.44 = f32[768,768]{1,0:T(8,128)S(1)} fusion(f32[128,512]{1,0:T(8,128)} %collective-permute-done.1, f32[512,512]{1,0:T(8,128)S(1)} %copy-done.3, f32[128,512]{1,0:T(8,128)} %collective-permute-done), kind=kOutput, calls=%fused_computation.47 | convolution fusion | flops 5445844992 | bytes 3932160 | tf_op jit(solution)/shard_map/dot_general | solution.py:40
  91.6 15.8 %fusion.53 = f32[768,768]{1,0:T(8,128)S(1)} fusion(f32[768,768]{1,0:T(8,128)S(1)} %fusion.44), kind=kOutput, calls=%fused_computation.55 | convolution fusion | flops 5441126400 | bytes 4718592 | tf_op jit(solution)/shard_map/dot_general | solution.py:40
  107.4 16.1 %fusion.56 = f32[768,768]{1,0:T(8,128)S(1)} fusion(f32[768,768]{1,0:T(8,128)S(1)} %fusion.44), kind=kOutput, calls=%fused_computation.56 | convolution fusion | flops 5441126400 | bytes 4718592 | tf_op jit(solution)/shard_map/dot_general | solution.py:40
  123.4 16.1 %fusion.45 = f32[768,768]{1,0:T(8,128)S(1)} fusion(f32[128,512]{1,0:T(8,128)} %collective-permute-done.1, f32[512,512]{1,0:T(8,128)S(1)} %copy-done.3, f32[128,512]{1,0:T(8,128)} %collective-permute-done), kind=kOutput, calls=%fused_computation.48 | convolution fusion | flops 5445844992 | bytes 3932160 | tf_op jit(solution)/shard_map/dot_general | solution.py:40
  139.6 15.9 %fusion.14 = f32[768,768]{1,0:T(8,128)S(1)} fusion(f32[768,768]{1,0:T(8,128)S(1)} %fusion.53, f32[768,768]{1,0:T(8,128)S(1)} %fusion.45), kind=kOutput, calls=%fused_computation.26 | convolution fusion | flops 5442306048 | bytes 7077888 | tf_op jit(solution)/shard_map/dot_general | solution.py:40
  155.5 26.0 %fusion.3 = (f32[768,768]{1,0:T(8,128)S(1)}, f32[768,768]{1,0:T(8,128)S(1)}) fusion(f32[768,768]{1,0:T(8,128)S(1)} %convolution_subtract_fusion, f32[768,768]{1,0:T(8,128)S(1)} %fusion.14, f32[768,768]{1,0:T(8,128)S(1)} %copy-done.1, f32[768]{0:T(1024)S(1)} %fusion.73, f32[]{:T(128)S(6)} %mul_shard_map.3, f32[768,768]{1,0:T(8,128)S(1)} %fusion.56, ...), kind=kOutput, calls=%fused_computation.14 | convolution fusion | flops 5450563584 | bytes 16518148 | tf_op jit(solution)/shard_map/dot_general | solution.py:40
  181.5 3.9 fusion.30
  185.4 3.9 fusion.28
  189.3 3.9 fusion.26
  193.2 3.9 fusion.32
  197.1 3.0 fusion.20
  200.1 4.1 fusion.103
  205.0 124.9 %all-gather.5.cloned.1.call-done = f32[4096,512]{1,0:T(8,128)} async-done(((f32[512,512]{1,0:T(8,128)}), f32[4096,512]{1,0:T(8,128)}) %all-gather.5.cloned.1.call-update) | async-done | bytes 8388624 | tf_op jit(solution)/shard_map/all_gather | solution.py:30
  331.2 123.9 %all-gather.7.cloned.1.call-done = f32[4096,512]{1,0:T(8,128)} async-done(((f32[512,512]{1,0:T(8,128)}), f32[4096,512]{1,0:T(8,128)}) %all-gather.7.cloned.1.call-update) | async-done | bytes 8388624 | tf_op jit(solution)/shard_map/all_gather | solution.py:30
  456.4 26.3 %while.23 = (s32[]{:T(128)}, f32[512,512]{1,0:T(8,128)S(1)}, f32[512,512]{1,0:T(8,128)}, f32[512,512]{1,0:T(8,128)S(1)}, f32[512,512]{1,0:T(8,128)S(1)}, /*index...) while((s32[]{:T(128)}, f32[512,512]{1,0:T(8,128)S(1)}, ...), condition=%wide.region_8.9_spmd.clone, body=%wide.region_7.8_spmd.clone.sunk | while | flops 1572870 | bytes 10485917 | solution.py:36
  456.4 3.5 fusion.115
  459.9 3.8 fusion.115
  463.7 3.8 fusion.115
  467.5 3.8 fusion.115
  471.3 3.8 fusion.115
  475.1 3.8 fusion.115
  478.9 3.8 fusion.115
  (33 shorter events, 14.9 us)
Async XLA Ops:
  7.2 322.7 %all-gather.5.cloned.1.call-start = ((), (), s32[]{:S(2)}) async-start(), calls=%async_computation | async-start | bytes 9437184 | tf_op jit(solution)/shard_map/all_gather | solution.py:30
  20.3 25.6 %copy-start.2 = (f32[512,512]{1,0:T(8,128)}, f32[512,512]{1,0:T(8,128)S(1)}, u32[]{:S(2)}) copy-start(f32[512,512]{1,0:T(8,128)S(1)} %subtract_divide_fusion) | copy-start | bytes 3145732
  21.3 54.1 %collective-permute-start = (f32[128,512]{1,0:T(8,128)}, f32[128,512]{1,0:T(8,128)}, u32[]{:S(2)}, u32[]{:S(2)}) collective-permute-start(f32[128,512]{1,0:T(8,128)} %get-tuple-element.267), channel_id=1, source_target_pairs={{0,8},{8,16},{16,24},{1,9},{9,17},{17,25},{2,10},{10,18},{18,26},{... | collective-permute-start | bytes 786440 | tf_op jit(solution)/shard_map/ppermute | solution.py:23
  25.1 20.8 %copy-start.4 = (f32[1,64,256]{2,1,0:T(8,128)S(1)}, f32[1,64,256]{2,1,0:T(8,128)}, u32[]{:S(2)}) copy-start(f32[1,64,256]{2,1,0:T(8,128)} %param.7) | copy-start | bytes 196612
  25.2 50.2 %collective-permute-start.1 = (f32[128,512]{1,0:T(8,128)}, f32[128,512]{1,0:T(8,128)}, u32[]{:S(2)}, u32[]{:S(2)}) collective-permute-start(f32[128,512]{1,0:T(8,128)} %get-tuple-element.268), channel_id=1, source_target_pairs={{8,0},{16,8},{24,16},{9,1},{17,9},{25,17},{10,2},{18,10},{26,18},{... | collective-permute-start | bytes 786440 | tf_op jit(solution)/shard_map/ppermute | solution.py:24
  65.7 4.3 copy-start.5
  71.3 4.0 copy-start.3
  139.6 16.0 %copy-start.1 = (f32[768,768]{1,0:T(8,128)S(1)}, f32[768,768]{1,0:T(8,128)}, u32[]{:S(2)}) copy-start(f32[768,768]{1,0:T(8,128)} %convolution_add_fusion) | copy-start | bytes 7077892
  155.5 26.0 %copy-start = (f32[768,768]{1,0:T(8,128)S(1)}, f32[768,768]{1,0:T(8,128)}, u32[]{:S(2)}) copy-start(f32[768,768]{1,0:T(8,128)} %fusion.7) | copy-start | bytes 7077892
  204.2 250.9 %all-gather.7.cloned.1.call-start = ((), (), s32[]{:S(2)}) async-start(), calls=%async_computation.1 | async-start | bytes 9437184 | tf_op jit(solution)/shard_map/all_gather | solution.py:30
Sparse Core Ops, SparseCore 0:
  204.4 125.4 all-gather.4
  332.0 123.1 all-gather.6
where the time goes:
time: 502 us; the launch traced here: 492 us
  waiting for transfers between devices  249 us (50%)
  matrix products  147 us (29%)
  other arithmetic  52 us (10%)
  between operations  20 us (4%)
  blocking collectives  13.3 us (3%)
  starting transfers between devices  6.11 us (1%)
    all_gather x2, waiting for transfers between devices, merged_2(): everything = jax.tree.map(lambda part: lax.all_gather(part, axis), shard)  249 us
    dot_general x18, matrix products, product(): jnp.dot(former, latter, precision=exact_mode, preferred_element_type=jnp....  147 us
    max x7, other arithmetic, combine(): jnp.maximum(jnp.minimum(former[0], latter[0]), jnp.maximum(former[1], lat...  26.3 us
  transfers between devices with their start and end apart: 4, of which 2 were waited for; matrix products, arithmetic and copies ran while one was open for 8% of the time, Pallas kernels for 0%

commit v1 on v0

v1 whole, which is shorter than its diff:
```python
import functools
import math

import jax
import jax.numpy as jnp
import ml_dtypes
import numpy as np
from jax import lax
from jax.experimental import pallas as pl
from jax.experimental.pallas import tpu as pltpu
from jax.sharding import PartitionSpec as P

TS = 512
TPL = 256
MARGIN = TPL // 2
EXT = TS + TPL
HALF = EXT // 2
FREQS = 400
GROUPS = 2
WAVELENGTH = 0.0197
AMPLITUDE = 0.07
ROOT = math.sqrt(3.0) / 2.0
MESH = pl.DeviceIdType.MESH
VMEM = pl.BlockSpec(memory_space=pltpu.VMEM)


def split_table(table):
    high = table.astype(ml_dtypes.bfloat16)
    low = (table - high.astype(np.float64)).astype(ml_dtypes.bfloat16)
    return high, low


@functools.lru_cache(None)
def tables():
    j, n = np.arange(HALF + 1)[:, None], np.arange(EXT)[None, :]
    angle = 2.0 * np.pi * (j * n % EXT) / EXT
    rows = np.zeros((2 * FREQS, EXT))
    rows[: HALF + 1], rows[FREQS : FREQS + HALF + 1] = np.cos(angle), -np.sin(angle)
    sample, a = np.arange(TPL)[:, None], np.arange(TPL)[None, :]
    cols = []
    for b in range(3):
        angle = 2.0 * np.pi * (sample * (3 * a + b) % EXT) / EXT
        re, im = np.cos(angle), -np.sin(angle)
        cols.append(np.block([[re, im], [-im, re]]))
    p, j = np.arange(TS)[:, None], np.arange(HALF)[None, :]
    angle = 2.0 * np.pi * (p * j % EXT) / EXT
    back_re, back_im = 2.0 * np.cos(angle), -2.0 * np.sin(angle)
    back_re[:, 0] = 1.0
    back_im[:, 0] = (-1.0) ** np.arange(TS)
    back = np.concatenate([back_re, back_im], axis=1)
    return split_table(rows) + split_table(np.stack(cols)) + split_table(back)


def split(value):
    high = value.astype(jnp.bfloat16)
    return high, (value - high.astype(jnp.float32)).astype(jnp.bfloat16)


def dot(a, b, contract=0):
    return lax.dot_general(
        a, b, (((1,), (contract,)), ((), ())), preferred_element_type=jnp.float32
    )


def dot3(a, b, contract=0):
    return dot(a[0], b[0], contract) + (dot(a[0], b[1], contract) + dot(a[1], b[0], contract))


def contrast_vectors(defocus):
    def chi(ids):
        signed = np.where(ids < HALF, ids, ids - EXT) / EXT
        return (math.pi * WAVELENGTH) * defocus * jnp.asarray(signed * signed, jnp.float32)

    k = 3 * np.arange(TPL)[None, :] + np.arange(3)[:, None]
    sign = jnp.asarray((-1.0) ** np.arange(TPL), jnp.float32)[None, :]
    chi_k = chi(k)
    along = jnp.stack([jnp.sin(chi_k) * sign, jnp.cos(chi_k) * sign], axis=1)
    j = np.minimum(np.arange(FREQS), HALF)
    chi_j = chi(j)
    wave = math.sqrt(1.0 - AMPLITUDE * AMPLITUDE)
    factor = -1.0 / (EXT * EXT)
    sin_j, cos_j = jnp.sin(chi_j), jnp.cos(chi_j)
    down = jnp.stack(
        [factor * (wave * cos_j - AMPLITUDE * sin_j), factor * (wave * sin_j + AMPLITUDE * cos_j)]
    )
    return along, down[:, :, None]


def gather_body(n, orients, image_ref, tmpl_ref, win_ref, normed_ref, stats, landed, gath,
                send_sem, recv_sem, tsend_sem, trecv_sem, hsend_sem, hrecv_sem):
    me = lax.axis_index("tile")
    orient = lax.axis_index("orient")
    lanes = orients // GROUPS
    share = TPL // n
    mine = lax.div(orient, lanes)
    partner = lax.rem(orient + lanes, orients)

    barrier = pltpu.get_barrier_semaphore()
    for step in range(n):
        other = lax.rem(me + step, n)
        if step:
            pl.semaphore_signal(barrier, inc=1, device_id={"tile": other, "orient": orient}, device_id_type=MESH)
        pl.semaphore_signal(barrier, inc=1, device_id={"tile": other, "orient": partner}, device_id_type=MESH)
    pl.semaphore_wait(barrier, 2 * n - 1)

    def tmpl_copy(step, away):
        other = lax.rem(me + step, n)
        where = partner if away else orient
        start = pl.multiple_of(me * share, share)
        return pltpu.make_async_remote_copy(
            src_ref=tmpl_ref.at[0],
            dst_ref=gath.at[mine, pl.ds(start, share)],
            send_sem=tsend_sem.at[away, step],
            recv_sem=trecv_sem.at[away, step],
            device_id={"tile": other, "orient": where},
            device_id_type=MESH,
        )

    def halo_copy(up):
        return pltpu.make_async_remote_copy(
            src_ref=image_ref.at[pl.ds(TS - MARGIN if up else 0, MARGIN)],
            dst_ref=landed.at[0 if up else 1],
            send_sem=hsend_sem.at[0 if up else 1],
            recv_sem=hrecv_sem.at[0 if up else 1],
            device_id={"tile": lax.rem(me + (1 if up else n - 1), n), "orient": orient},
            device_id_type=MESH,
        )

    tcopies = [tmpl_copy(s, a) for a in (1, 0) for s in range(n) if s or a]
    for copy in tcopies:
        copy.start()
    halos = [halo_copy(True), halo_copy(False)]
    for copy in halos:
        copy.start()

    image = image_ref[...]
    total = jnp.sum(image)
    squares = jnp.sum(image * image)
    lane = lax.broadcasted_iota(jnp.int32, (8, 128), 1)
    stats[me] = jnp.where(lane == 0, total, jnp.where(lane == 1, squares, 0.0))
    scopies = []
    for step in range(1, n):
        copy = pltpu.make_async_remote_copy(
            src_ref=stats.at[me],
            dst_ref=stats.at[me],
            send_sem=send_sem.at[step],
            recv_sem=recv_sem.at[step],
            device_id={"tile": lax.rem(me + step, n), "orient": orient},
            device_id_type=MESH,
        )
        copy.start()
        scopies.append(copy)
    gath[mine, pl.ds(pl.multiple_of(me * share, share), share)] = tmpl_ref[0]
    for copy in scopies:
        copy.wait()
    sums = stats[0]
    for step in range(1, n):
        sums = sums + stats[step]
    pixels = float(TS * TS * n)
    centre = jnp.sum(jnp.where(lane == 0, sums, 0.0)) / (8.0 * pixels)
    square = jnp.sum(jnp.where(lane == 1, sums, 0.0)) / (8.0 * pixels)
    centre = jnp.full((1, TS), centre, jnp.float32)
    inverse = lax.rsqrt(square - centre * centre + 1e-05)
    win_ref[MARGIN : MARGIN + TS] = (image - centre) * inverse
    for copy in halos:
        copy.wait()
    win_ref[:MARGIN] = jnp.where(me > 0, (landed[0] - centre) * inverse, 0.0)
    win_ref[MARGIN + TS :] = jnp.where(me < n - 1, (landed[1] - centre) * inverse, 0.0)
    for copy in tcopies:
        copy.wait()
    for g in range(GROUPS):
        tmpl = gath[g]
        centred = tmpl - jnp.sum(tmpl) / (TPL * TPL)
        mean_square = jnp.full((1, TPL), jnp.sum(centred * centred) / (TPL * TPL), jnp.float32)
        normed_ref[g] = centred * (lax.rsqrt(mean_square + 1e-06) * (1.0 / TPL))


def score_body(orients, win_ref, normed_ref, along_ref, down_ref, rows_h, rows_l, cols_h, cols_l,
               back_h, back_l, out_ref, half_spec, u_h, u_l, wide, v_h, v_l, backs):
    lanes = orients // GROUPS
    mine = lax.div(lax.axis_index("orient"), lanes)
    part = TS // GROUPS

    half_spec[...] = dot3((rows_h[...], rows_l[...]), split(win_ref[...]))
    re0, re1 = half_spec[:FREQS, :TPL], half_spec[:FREQS, TPL:]
    im0, im1 = half_spec[FREQS:, :TPL], half_spec[FREQS:, TPL:]
    joined = (
        (re0 + re1, im0 + im1),
        (0.5 * re0 + ROOT * im0 - re1, 0.5 * im0 - ROOT * re0 - im1),
        (re1 - 0.5 * re0 + ROOT * im0, im1 - 0.5 * im0 - ROOT * re0),
    )
    for b, (re, im) in enumerate(joined):
        u_h[b, :, :TPL], u_l[b, :, :TPL] = split(re)
        u_h[b, :, TPL:], u_l[b, :, TPL:] = split(im)

    def forward(b, carry):
        spec = dot3((u_h[b], u_l[b]), (cols_h[b], cols_l[b]))
        contrast = along_ref[b, 0:1] * down_ref[0] + along_ref[b, 1:2] * down_ref[1]
        wide[b, :, :TPL] = spec[:, :TPL] * contrast
        wide[b, :, TPL:] = spec[:, TPL:] * contrast
        return carry

    lax.fori_loop(0, 3, forward, 0)

    def one(g, carry):
        first = dot3((rows_h[:, :TPL], rows_l[:, :TPL]), split(normed_ref[g]))
        v_h[:, :TPL], v_l[:, :TPL] = split(first[:FREQS])
        v_h[:, TPL:], v_l[:, TPL:] = split(first[FREQS:])

        def branch(b, carry):
            spec = dot3((v_h[...], v_l[...]), (cols_h[b], cols_l[b]))
            w_re, w_im = wide[b, :, :TPL], wide[b, :, TPL:]
            t_re, t_im = spec[:, :TPL], spec[:, TPL:]
            prod = jnp.concatenate([w_re * t_re + w_im * t_im, w_im * t_re - w_re * t_im], axis=1)
            backs[b] = dot3(split(prod), (cols_h[b], cols_l[b]), 1)
            return carry

        lax.fori_loop(0, 3, branch, 0)
        e_re, e_im = [backs[b, :, :TPL] for b in range(3)], [backs[b, :, TPL:] for b in range(3)]
        sum_re, sum_im = e_re[1] + e_re[2], e_im[1] + e_im[2]
        out_re = jnp.concatenate(
            [e_re[0] + sum_re, e_re[0] - 0.5 * sum_re - ROOT * (e_im[1] - e_im[2])], axis=1
        )
        out_im = jnp.concatenate(
            [e_im[0] + sum_im, e_im[0] - 0.5 * sum_im + ROOT * (e_re[1] - e_re[2])], axis=1
        )
        top = lax.broadcasted_iota(jnp.int32, (HALF, 1), 0) == 0
        out_im = jnp.where(top, out_re[HALF : HALF + 1], out_im[:HALF])
        packed = split(jnp.concatenate([out_re[:HALF], out_im], axis=0))
        own = pl.ds(pl.multiple_of(mine * part, part), part)
        out_ref[g] = dot3((back_h[own], back_l[own]), packed)
        return carry

    lax.fori_loop(0, GROUPS, one, 0)


def merge_body(orients, scores_ref, best_ref, second_ref, mean_ref, var_ref, landed, send_sem, recv_sem):
    lanes = orients // GROUPS
    share = TS // orients
    orient = lax.axis_index("orient")
    group = lax.div(orient, lanes)
    lo = lax.rem(orient, lanes)

    def place(step):
        return group * lanes + lax.rem(lo + step, lanes)

    barrier = pltpu.get_barrier_semaphore()
    for step in range(1, lanes):
        pl.semaphore_signal(barrier, inc=1, device_id={"orient": place(step)}, device_id_type=MESH)
    pl.semaphore_wait(barrier, lanes - 1)
    copies = []
    for g in range(GROUPS):
        for step in range(1, lanes):
            start = pl.multiple_of(lax.rem(lo + step, lanes) * share, share)
            copy = pltpu.make_async_remote_copy(
                src_ref=scores_ref.at[g, pl.ds(start, share)],
                dst_ref=landed.at[g, step],
                send_sem=send_sem.at[g, step],
                recv_sem=recv_sem.at[g, step],
                device_id={"orient": place(step)},
                device_id_type=MESH,
            )
            copy.start()
            copies.append(copy)
    own = pl.ds(pl.multiple_of(lo * share, share), share)
    first, other = scores_ref[0, own], scores_ref[1, own]
    best, second = jnp.maximum(first, other), jnp.minimum(first, other)
    total, squares = first + other, first * first + other * other
    for copy in copies:
        copy.wait()
    for step in range(1, lanes):
        for g in range(GROUPS):
            score = landed[g, step]
            second = jnp.maximum(second, jnp.minimum(best, score))
            best = jnp.maximum(best, score)
            total = total + score
            squares = squares + score * score
    mean = total / orients
    best_ref[...] = best
    second_ref[...] = second
    mean_ref[...] = mean
    var_ref[...] = squares / orients - mean * mean


def per_device(n, orients, micrograph, templates, defocus_values, defocus_group):
    f32, b16 = jnp.float32, jnp.bfloat16
    lanes, share = orients // GROUPS, TS // orients
    group_ids = lax.iota(jnp.int32, defocus_values.shape[0])
    defocus = jnp.sum(jnp.where(group_ids == defocus_group[0], defocus_values, 0.0))
    along, down = contrast_vectors(defocus)
    dma = pltpu.SemaphoreType.DMA
    window, normed = pl.pallas_call(
        functools.partial(gather_body, n, orients),
        out_shape=(
            jax.ShapeDtypeStruct((EXT, TS), f32),
            jax.ShapeDtypeStruct((GROUPS, TPL, TPL), f32),
        ),
        in_specs=[VMEM] * 2,
        out_specs=(VMEM, VMEM),
        scratch_shapes=[
            pltpu.VMEM((n, 8, 128), f32),
            pltpu.VMEM((2, MARGIN, TS), f32),
            pltpu.VMEM((GROUPS, TPL, TPL), f32),
            dma((n,)), dma((n,)), dma((2, n)), dma((2, n)), dma((2,)), dma((2,)),
        ],
        compiler_params=pltpu.CompilerParams(
            collective_id=0, has_side_effects=True, vmem_limit_bytes=16 * 2**20
        ),
        name="gather_normalise",
    )(micrograph, templates)
    scores = pl.pallas_call(
        functools.partial(score_body, orients),
        out_shape=jax.ShapeDtypeStruct((GROUPS, TS // GROUPS, TS), f32),
        in_specs=[VMEM] * 10,
        out_specs=VMEM,
        scratch_shapes=[
            pltpu.VMEM((2 * FREQS, TS), f32),
            pltpu.VMEM((3, FREQS, TS), b16),
            pltpu.VMEM((3, FREQS, TS), b16),
            pltpu.VMEM((3, FREQS, TS), f32),
            pltpu.VMEM((FREQS, TS), b16),
            pltpu.VMEM((FREQS, TS), b16),
            pltpu.VMEM((3, FREQS, TS), f32),
        ],
        compiler_params=pltpu.CompilerParams(vmem_limit_bytes=56 * 2**20),
        name="score",
    )(window, normed, along, down, *(jnp.asarray(t) for t in tables()))
    out = jax.ShapeDtypeStruct((share, TS), f32)
    return pl.pallas_call(
        functools.partial(merge_body, orients),
        out_shape=(out,) * 4,
        in_specs=[VMEM],
        out_specs=(VMEM,) * 4,
        scratch_shapes=[
            pltpu.VMEM((GROUPS, lanes, share, TS), f32),
            dma((GROUPS, lanes)),
            dma((GROUPS, lanes)),
        ],
        compiler_params=pltpu.CompilerParams(
            collective_id=1, has_side_effects=True, vmem_limit_bytes=16 * 2**20
        ),
        name="exchange_merge",
    )(scores)


def solution(mesh):
    placed = (P("tile", None), P("orient", "tile", None), P(), P("tile"))
    return jax.shard_map(
        functools.partial(per_device, mesh.shape["tile"], mesh.shape["orient"]),
        mesh=mesh,
        in_specs=placed,
        out_specs=(P(("tile", "orient"), None),) * 4,
        check_vma=False,
    )
```

time: 502 us -> 70.4 us (0.14); the launches traced: 492 us -> 69.6 us
  waiting for transfers between devices: 249 us -> 0 us
  matrix products: 147 us -> 0 us
  Pallas kernels: 0 us -> 55.5 us
  other arithmetic: 52 us -> 3.36 us
  between operations: 20 us -> 1.99 us
  blocking collectives: 13.3 us -> 0 us
  starting transfers between devices: 6.11 us -> 0 us
    all_gather x2 -> x0, waiting for transfers between devices: 249 us -> none  [merged_2(): everything = jax.tree.map(lambda part: lax.all_gather(part, axis), shard)]
    dot_general x18 -> x0, matrix products: 147 us -> none  [product(): jnp.dot(former, latter, precision=exact_mode, preferred_element_type=jnp....]
    pallas_call x0 -> x3, Pallas kernels: none -> 55.5 us  [the longest x1 21.5 us: per_device(): pl.pallas_call(functools.partial(score_body, orients), out_shape=jax.Shap...]
    max x7 -> x0, other arithmetic: 26.3 us -> none  [combine(): jnp.maximum(jnp.minimum(former[0], latter[0]), jnp.maximum(former[1], lat...]
    cos x1 -> x0, other arithmetic: 9.75 us -> none  [fourier_tables(): return (jnp.cos(angles), jnp.sin(angles))]
    sin x1 -> x0, other arithmetic: 8.88 us -> none  [fourier_tables(): return (jnp.cos(angles), jnp.sin(angles))]
    unnamed x13 -> x14, local copies, waits for them, and re-layouts: 0.1 us -> 7.87 us
    psum x1 -> x0, blocking collectives: 6.99 us -> none  [per_device(): totals = lax.psum((local_sums[0], local_sums[1]), 'tile')]
  transfers between devices with their start and end apart: 4 -> 0, of which waited for: 2 -> 0; matrix products, arithmetic and copies ran while one was open for 8% -> 0% of each run, Pallas kernels for 0% -> 0%
where the time goes in v1:
time: 70.4 us; the launch traced here: 69.6 us
  Pallas kernels  55.5 us (79%)
  local copies, waits for them, and re-layouts  8.83 us (13%)
  other arithmetic  3.36 us (5%)
  between operations  1.99 us (3%)
    pallas_call x1, Pallas kernels, per_device(): pl.pallas_call(functools.partial(score_body, orients), out_shape=jax.Shap...  21.5 us
    pallas_call x1, Pallas kernels, per_device(): pl.pallas_call(functools.partial(gather_body, n, orients), out_shape=(jax...  18.7 us
    pallas_call x1, Pallas kernels, per_device(): pl.pallas_call(functools.partial(merge_body, orients), out_shape=(out,) *...  15.3 us
    unnamed x14, local copies, waits for them, and re-layouts  7.87 us

profile of v1, /device:TPU:1, one launch (start us, length us, event | category | flops | bytes accessed | tf_op | source)
XLA Modules:
  0.0 69.6 jit_solution(558900459356503077)
XLA Ops:
  1.3 1.3 %fusion.11 = f32[]{:T(128)} fusion(f32[4]{0:T(128)} %param.15, s32[]{:T(128)} %bitcast.7), kind=kLoop, calls=%fused_computation.18 | loop fusion | flops 11 | bytes 24 | tf_op jit(solution)/shard_map/reduce_sum | solution.py:289
  3.2 0.7 %fusion.8 = (f32[400]{0:T(512)S(1)}, f32[400]{0:T(512)S(1)}) fusion(f32[400]{0:T(512)} %constant.30.clone, f32[]{:T(128)S(6)} %mul.48), kind=kLoop, calls=%fused_computation.14 | loop fusion | flops 3600 | bytes 4804 | tf_op jit(solution)/shard_map/mul | solution.py:84
  3.9 0.8 %fusion.1 = (f32[3,1,256]{2,0,1:T(4,128)S(1)}, f32[3,256]{1,0:T(4,128)S(1)}) fusion(f32[3,256]{1,0:T(4,128)} %constant.29.clone, f32[256]{0:T(256)} %constant.28.clone, f32[]{:T(128)S(6)} %mul.48), kind=kLoop, calls=%fused_computation.4 | loop fusion | flops 2304 | bytes 10244 | tf_op jit(solution)/shard_map/stack | solution.py:77
  4.7 0.6 pad_maximum_fusion.along_ref
  5.3 1.0 %copy.19.down_ref = f32[2,400,1]{2,1,0:T(8,128)} copy(f32[2,400,1]{1,0,2:T(2,128)S(1)} %maximum_bitcast_fusion) | data formatting | bytes 6400 | tf_op jit(solution)/shard_map/broadcast_in_dim | solution.py:86
  6.3 0.0 copy-start.2
  6.3 1.2 %copy-done.2 = f32[512,512]{1,0:T(8,128)S(1)} copy-done((f32[512,512]{1,0:T(8,128)S(1)}, f32[512,512]{1,0:T(8,128)}, u32[]{:S(2)}) %copy-start.2) | copy-done | bytes 1048600
  7.5 0.0 copy-start.4
  7.5 0.8 %copy-done.4 = f32[1,64,256]{2,1,0:T(8,128)S(1)} copy-done((f32[1,64,256]{2,1,0:T(8,128)S(1)}, f32[1,64,256]{2,1,0:T(8,128)}, u32[]{:S(2)}) %copy-start.4) | copy-done | bytes 65560
  8.3 18.7 %gather_normalise.1 = (f32[768,512]{1,0:T(8,128)S(1)}, f32[2,256,256]{2,1,0:T(8,128)S(1)}) custom-call(f32[512,512]{1,0:T(8,128)S(1)} %copy-done.2, f32[1,64,256]{2,1,0:T(8,128)S(1)} %copy-done.4), custom_call_target="tpu_custom_call" | custom-call | tf_op jit(solution)/shard_map/gather_normalise/pallas_call | solution.py:292
  27.0 0.0 copy-start.1
  27.1 1.1 %copy-done.1 = f32[768,512]{1,0:T(8,128)} copy-done((f32[768,512]{1,0:T(8,128)}, f32[768,512]{1,0:T(8,128)S(1)}, u32[]{:S(2)}) %copy-start.1) | copy-done | bytes 1572888
  28.2 0.0 copy-start.3
  28.2 0.8 %copy-done.3 = f32[2,256,256]{2,1,0:T(8,128)} copy-done((f32[2,256,256]{2,1,0:T(8,128)}, f32[2,256,256]{2,1,0:T(8,128)S(1)}, u32[]{:S(2)}) %copy-start.3) | copy-done | bytes 524312
  29.0 21.5 %score.1.scores_ref = f32[2,256,512]{2,1,0:T(8,128)} custom-call(f32[768,512]{1,0:T(8,128)} %copy-done.1, f32[2,256,256]{2,1,0:T(8,128)} %copy-done.3, f32[3,2,256]{2,1,0:T(2,128)} %pad_maximum_fusion.along_ref, f32[2,400,1]{2,1,0:T(8,128)} %copy.19.down_ref, bf16[800,768]{1,0:T(8,128)(2,1)} %constant.31.clone.rows_h, ...), custom_call_target="tpu_custom_call" | custom-call | tf_op jit(solution)/shard_map/score/pallas_call | solution.py:311
  50.5 0.0 copy-start
  50.5 1.2 %copy-done = f32[2,256,512]{2,1,0:T(8,128)S(1)} copy-done((f32[2,256,512]{2,1,0:T(8,128)S(1)}, f32[2,256,512]{2,1,0:T(8,128)}, u32[]{:S(2)}) %copy-start) | copy-done | bytes 1048600
  51.7 15.3 %exchange_merge.1 = (f32[64,512]{1,0:T(8,128)S(1)}, f32[64,512]{1,0:T(8,128)S(1)}, f32[64,512]{1,0:T(8,128)S(1)}, f32[64,512]{1,0:T(8,128)S(1)}) custom-call(f32[2,256,512]{2,1,0:T(8,128)S(1)} %copy-done), custom_call_target="tpu_custom_call" | custom-call | tf_op jit(solution)/shard_map/exchange_merge/pallas_call | solution.py:329
  67.0 0.7 copy.25
  67.7 0.7 copy.26
  68.3 0.7 copy.27
  69.0 0.7 copy.28
  (3 shorter events, 0.0 us)
Async XLA Ops:
  6.3 1.2 %copy-start.2 = (f32[512,512]{1,0:T(8,128)S(1)}, f32[512,512]{1,0:T(8,128)}, u32[]{:S(2)}) copy-start(f32[512,512]{1,0:T(8,128)} %image_ref.1) | copy-start | bytes 3145732
  7.5 0.8 %copy-start.4 = (f32[1,64,256]{2,1,0:T(8,128)S(1)}, f32[1,64,256]{2,1,0:T(8,128)}, u32[]{:S(2)}) copy-start(f32[1,64,256]{2,1,0:T(8,128)} %tmpl_ref.1) | copy-start | bytes 196612
  27.0 1.2 %copy-start.1 = (f32[768,512]{1,0:T(8,128)}, f32[768,512]{1,0:T(8,128)S(1)}, u32[]{:S(2)}) copy-start(f32[768,512]{1,0:T(8,128)S(1)} %get-tuple-element.6.win_ref) | copy-start | bytes 4718596
  28.2 0.8 %copy-start.3 = (f32[2,256,256]{2,1,0:T(8,128)}, f32[2,256,256]{2,1,0:T(8,128)S(1)}, u32[]{:S(2)}) copy-start(f32[2,256,256]{2,1,0:T(8,128)S(1)} %get-tuple-element.7.normed_ref) | copy-start | bytes 1572868
  50.5 1.2 %copy-start = (f32[2,256,512]{2,1,0:T(8,128)S(1)}, f32[2,256,512]{2,1,0:T(8,128)}, u32[]{:S(2)}) copy-start(f32[2,256,512]{2,1,0:T(8,128)} %score.1.scores_ref) | copy-start | bytes 3145732

commit v2 on v1

v2 whole, which is shorter than its diff:
```python
import functools
import math

import jax
import jax.numpy as jnp
import ml_dtypes
import numpy as np
from jax import lax
from jax.experimental import pallas as pl
from jax.experimental.pallas import tpu as pltpu
from jax.sharding import PartitionSpec as P

TS = 512
TPL = 256
MARGIN = TPL // 2
EXT = TS + TPL
HALF = EXT // 2
FREQS = 400
GROUPS = 2
WAVELENGTH = 0.0197
AMPLITUDE = 0.07
ROOT = math.sqrt(3.0) / 2.0
MESH = pl.DeviceIdType.MESH
VMEM = pl.BlockSpec(memory_space=pltpu.VMEM)


def split_table(table):
    high = table.astype(ml_dtypes.bfloat16)
    low = (table - high.astype(np.float64)).astype(ml_dtypes.bfloat16)
    return high, low


@functools.lru_cache(None)
def tables():
    j, n = np.arange(HALF + 1)[:, None], np.arange(EXT)[None, :]
    angle = 2.0 * np.pi * (j * n % EXT) / EXT
    rows = np.zeros((2 * FREQS, EXT))
    rows[: HALF + 1], rows[FREQS : FREQS + HALF + 1] = np.cos(angle), -np.sin(angle)
    sample, a = np.arange(TPL)[:, None], np.arange(TPL)[None, :]
    cols = []
    for b in range(3):
        angle = 2.0 * np.pi * (sample * (3 * a + b) % EXT) / EXT
        re, im = np.cos(angle), -np.sin(angle)
        cols.append(np.block([[re, im], [-im, re]]))
    p, j = np.arange(TS)[:, None], np.arange(HALF)[None, :]
    angle = 2.0 * np.pi * (p * j % EXT) / EXT
    back_re, back_im = 2.0 * np.cos(angle), -2.0 * np.sin(angle)
    back_re[:, 0] = 1.0
    back_im[:, 0] = (-1.0) ** np.arange(TS)
    back = np.concatenate([back_re, back_im], axis=1)
    return split_table(rows) + split_table(np.stack(cols)) + split_table(back)


def split(value):
    high = value.astype(jnp.bfloat16)
    return high, (value - high.astype(jnp.float32)).astype(jnp.bfloat16)


def dot(a, b, contract=0):
    return lax.dot_general(
        a, b, (((1,), (contract,)), ((), ())), preferred_element_type=jnp.float32
    )


def dot3(a, b, contract=0):
    return dot(a[0], b[0], contract) + (dot(a[0], b[1], contract) + dot(a[1], b[0], contract))


def circular(turns):
    half = (turns - jnp.round(turns)) * math.pi
    square = half * half
    sine = jnp.full_like(half, 1.0 / math.factorial(13))
    cosine = jnp.full_like(half, -1.0 / math.factorial(14))
    for k in range(5, -1, -1):
        sine = sine * square + (-1.0) ** k / math.factorial(2 * k + 1)
    for k in range(6, -1, -1):
        cosine = cosine * square + (-1.0) ** k / math.factorial(2 * k)
    sine = sine * half
    return 2.0 * sine * cosine, 1.0 - 2.0 * sine * sine


def contrast_vectors(defocus):
    a = lax.broadcasted_iota(jnp.int32, (8, TPL), 1)
    b = lax.broadcasted_iota(jnp.int32, (8, TPL), 0)
    k = 3 * a + b
    k = jnp.where(k < HALF, k, k - EXT).astype(jnp.float32) * (1.0 / EXT)
    j = jnp.minimum(lax.broadcasted_iota(jnp.int32, (FREQS, 128), 0), HALF)
    j = j.astype(jnp.float32) * (1.0 / EXT)
    sign = (1 - 2 * (a & 1)).astype(jnp.float32)
    rate = (WAVELENGTH / 2.0) * defocus
    sin_k, cos_k = circular(rate * (k * k))
    sin_j, cos_j = circular(rate * (j * j))
    wave = math.sqrt(1.0 - AMPLITUDE * AMPLITUDE)
    factor = -1.0 / (EXT * EXT)
    return (
        (sin_k * sign, cos_k * sign),
        (factor * (wave * cos_j - AMPLITUDE * sin_j), factor * (wave * sin_j + AMPLITUDE * cos_j)),
    )


def body(n, orients, values_ref, group_ref, image_ref, tmpl_ref, *rest):
    hbm_tables, rest = rest[:6], rest[6:]
    (out_ref, rows_h, rows_l, cols_h, cols_l, back_h, back_l, stats, halo, gath, win_h, win_l,
     along, down, half_spec, u_h, u_l, wide, v_h, v_l, backs, scores, landed,
     table_sem, stat_send, stat_recv, halo_send, halo_recv, far_send, far_recv,
     near_send, near_recv, pass_send, pass_recv, score_send, score_recv) = rest
    me, orient = lax.axis_index("tile"), lax.axis_index("orient")
    lanes, share, shard = orients // GROUPS, TS // orients, TPL // n
    mine, lo = lax.div(orient, lanes), lax.rem(orient, lanes)
    partner = lax.rem(orient + lanes, orients)
    own_shard = pl.ds(pl.multiple_of(me * shard, shard), shard)

    def tile(step):
        return {"tile": lax.rem(me + step, n), "orient": orient}

    def lane(step):
        return {"tile": me, "orient": mine * lanes + lax.rem(lo + step, lanes)}

    across = {"tile": me, "orient": partner}

    def send(src, dst, send_sem, recv_sem, where):
        copy = pltpu.make_async_remote_copy(
            src_ref=src, dst_ref=dst, send_sem=send_sem, recv_sem=recv_sem,
            device_id=where, device_id_type=MESH,
        )
        copy.start()
        return copy

    barrier = pltpu.get_barrier_semaphore()
    for step in range(1, n):
        pl.semaphore_signal(barrier, inc=1, device_id=tile(step), device_id_type=MESH)
    pl.semaphore_signal(barrier, inc=1, device_id=across, device_id_type=MESH)
    for step in range(1, lanes):
        pl.semaphore_signal(barrier, inc=1, device_id=lane(step), device_id_type=MESH)

    held = (rows_h, rows_l, cols_h, cols_l, back_h, back_l)
    loads = [pltpu.make_async_copy(src, dst, table_sem.at[i])
             for i, (src, dst) in enumerate(zip(hbm_tables, held))]
    for load in loads:
        load.start()

    image = image_ref[...]
    total = jnp.sum(image)
    squares = jnp.sum(image * image)
    spot = lax.broadcasted_iota(jnp.int32, (8, 128), 1)
    stats[me] = jnp.where(spot == 0, total, jnp.where(spot == 1, squares, 0.0))
    gath[mine, own_shard] = tmpl_ref[0]

    pl.semaphore_wait(barrier, (n - 1) + 1 + (lanes - 1))
    stat_copies = [
        send(stats.at[me], stats.at[me], stat_send.at[s], stat_recv.at[s], tile(s))
        for s in range(1, n)
    ]
    halo_copies = [
        send(image_ref.at[pl.ds(TS - MARGIN, MARGIN)], halo.at[0], halo_send.at[0], halo_recv.at[0], tile(1)),
        send(image_ref.at[pl.ds(0, MARGIN)], halo.at[1], halo_send.at[1], halo_recv.at[1], tile(n - 1)),
    ]
    far_copy = send(tmpl_ref.at[0], gath.at[mine, own_shard], far_send, far_recv, across)
    near_copies = [
        send(tmpl_ref.at[0], gath.at[mine, own_shard], near_send.at[s], near_recv.at[s], tile(s))
        for s in range(1, n)
    ]

    wave_along, wave_down = contrast_vectors(values_ref[group_ref[0]])
    for i in range(2):
        along[i] = wave_along[i]
        down[i] = wave_down[i]

    for copy in stat_copies:
        copy.wait()
    sums = stats[0]
    for step in range(1, n):
        sums = sums + stats[step]
    pixels = float(TS * TS * n)
    centre = jnp.sum(jnp.where(spot == 0, sums, 0.0)) / (8.0 * pixels)
    square = jnp.sum(jnp.where(spot == 1, sums, 0.0)) / (8.0 * pixels)
    centre = jnp.full((1, TS), centre, jnp.float32)
    inverse = lax.rsqrt(square - centre * centre + 1e-05)
    inner = pl.ds(MARGIN, TS)
    win_h[inner], win_l[inner] = split((image_ref[...] - centre) * inverse)
    for copy in halo_copies:
        copy.wait()
    for i, (there, where) in enumerate(((me > 0, 0), (me < n - 1, MARGIN + TS))):
        edge = jnp.where(there, (halo[i] - centre) * inverse, 0.0)
        win_h[pl.ds(where, MARGIN)], win_l[pl.ds(where, MARGIN)] = split(edge)

    far_copy.wait()
    far_shard = gath.at[1 - mine, own_shard]
    pass_copies = [
        send(far_shard, far_shard, pass_send.at[s], pass_recv.at[s], tile(s)) for s in range(1, n)
    ]

    for load in loads:
        load.wait()
    half_spec[...] = dot3((rows_h[...], rows_l[...]), (win_h[...], win_l[...]))
    re0, re1 = half_spec[:FREQS, :TPL], half_spec[:FREQS, TPL:]
    im0, im1 = half_spec[FREQS:, :TPL], half_spec[FREQS:, TPL:]
    joined = (
        (re0 + re1, im0 + im1),
        (0.5 * re0 + ROOT * im0 - re1, 0.5 * im0 - ROOT * re0 - im1),
        (re1 - 0.5 * re0 + ROOT * im0, im1 - 0.5 * im0 - ROOT * re0),
    )
    for b, (re, im) in enumerate(joined):
        u_h[b, :, :TPL], u_l[b, :, :TPL] = split(re)
        u_h[b, :, TPL:], u_l[b, :, TPL:] = split(im)

    for b in range(3):
        spec = dot3((u_h[b], u_l[b]), (cols_h[b], cols_l[b]))
        for at in range(0, TPL, 128):
            here = slice(at, at + 128)
            contrast = along[0, b : b + 1, here] * down[0] + along[1, b : b + 1, here] * down[1]
            wide[b, :, at : at + 128] = spec[:, at : at + 128] * contrast
            wide[b, :, TPL + at : TPL + at + 128] = spec[:, TPL + at : TPL + at + 128] * contrast

    score_copies = []
    for turn in range(GROUPS):
        for copy in near_copies if turn == 0 else pass_copies:
            copy.wait()
        tmpl = gath[mine if turn == 0 else 1 - mine]
        centred = tmpl - jnp.sum(tmpl) / (TPL * TPL)
        mean_square = jnp.full((1, TPL), jnp.sum(centred * centred) / (TPL * TPL), jnp.float32)
        normed = centred * (lax.rsqrt(mean_square + 1e-06) * (1.0 / TPL))
        first = dot3((rows_h[:, :TPL], rows_l[:, :TPL]), split(normed))
        v_h[:, :TPL], v_l[:, :TPL] = split(first[:FREQS])
        v_h[:, TPL:], v_l[:, TPL:] = split(first[FREQS:])

        def branch(b, carry):
            spec = dot3((v_h[...], v_l[...]), (cols_h[b], cols_l[b]))
            w_re, w_im = wide[b, :, :TPL], wide[b, :, TPL:]
            t_re, t_im = spec[:, :TPL], spec[:, TPL:]
            prod = jnp.concatenate([w_re * t_re + w_im * t_im, w_im * t_re - w_re * t_im], axis=1)
            backs[b] = dot3(split(prod), (cols_h[b], cols_l[b]), 1)
            return carry

        lax.fori_loop(0, 3, branch, 0)
        e_re, e_im = [backs[b, :, :TPL] for b in range(3)], [backs[b, :, TPL:] for b in range(3)]
        sum_re, sum_im = e_re[1] + e_re[2], e_im[1] + e_im[2]
        out_re = jnp.concatenate(
            [e_re[0] + sum_re, e_re[0] - 0.5 * sum_re - ROOT * (e_im[1] - e_im[2])], axis=1
        )
        out_im = jnp.concatenate(
            [e_im[0] + sum_im, e_im[0] - 0.5 * sum_im + ROOT * (e_re[1] - e_re[2])], axis=1
        )
        top = lax.broadcasted_iota(jnp.int32, (HALF, 1), 0) == 0
        out_im = jnp.where(top, out_re[HALF : HALF + 1], out_im[:HALF])
        packed = split(jnp.concatenate([out_re[:HALF], out_im], axis=0))
        part = TS // GROUPS
        own = pl.ds(pl.multiple_of(mine * part, part), part)
        scores[turn] = dot3((back_h[own], back_l[own]), packed)
        for step in range(1, lanes):
            start = pl.multiple_of(lax.rem(lo + step, lanes) * share, share)
            score_copies.append(send(
                scores.at[turn, pl.ds(start, share)], landed.at[turn, step],
                score_send.at[turn, step], score_recv.at[turn, step], lane(step),
            ))

    own = pl.ds(pl.multiple_of(lo * share, share), share)
    first, other = scores[0, own], scores[1, own]
    best, second = jnp.maximum(first, other), jnp.minimum(first, other)
    total, squares = first + other, first * first + other * other
    for copy in score_copies:
        copy.wait()
    for g in range(GROUPS):
        for step in range(1, lanes):
            score = landed[g, step]
            second = jnp.maximum(second, jnp.minimum(best, score))
            best = jnp.maximum(best, score)
            total = total + score
            squares = squares + score * score
    out_ref[0] = best
    out_ref[1] = second
    out_ref[2] = total
    out_ref[3] = squares


def finish(orients, merged_ref, best_ref, second_ref, mean_ref, var_ref):
    best_ref[...] = merged_ref[0]
    second_ref[...] = merged_ref[1]
    mean = merged_ref[2] / orients
    mean_ref[...] = mean
    var_ref[...] = merged_ref[3] / orients - mean * mean


def per_device(n, orients, micrograph, templates, defocus_values, defocus_group):
    f32, b16 = jnp.float32, jnp.bfloat16
    lanes, share = orients // GROUPS, TS // orients
    dma, vmem = pltpu.SemaphoreType.DMA, pltpu.VMEM
    held = [jnp.asarray(t) for t in tables()]
    smem = pl.BlockSpec(memory_space=pltpu.SMEM)
    anywhere = pl.BlockSpec(memory_space=pl.ANY)
    merged = pl.pallas_call(
        functools.partial(body, n, orients),
        out_shape=jax.ShapeDtypeStruct((4, share, TS), f32),
        in_specs=[smem, smem, VMEM, VMEM] + [anywhere] * 6,
        out_specs=VMEM,
        scratch_shapes=[vmem(t.shape, b16) for t in held] + [
            vmem((n, 8, 128), f32),
            vmem((2, MARGIN, TS), f32),
            vmem((GROUPS, TPL, TPL), f32),
            vmem((EXT, TS), b16),
            vmem((EXT, TS), b16),
            vmem((2, 8, TPL), f32),
            vmem((2, FREQS, 128), f32),
            vmem((2 * FREQS, TS), f32),
            vmem((3, FREQS, TS), b16),
            vmem((3, FREQS, TS), b16),
            vmem((3, FREQS, TS), f32),
            vmem((FREQS, TS), b16),
            vmem((FREQS, TS), b16),
            vmem((3, FREQS, TS), f32),
            vmem((GROUPS, TS // GROUPS, TS), f32),
            vmem((GROUPS, lanes, share, TS), f32),
            dma((6,)),
            dma((n,)), dma((n,)), dma((2,)), dma((2,)), dma, dma,
            dma((n,)), dma((n,)), dma((n,)), dma((n,)),
            dma((GROUPS, lanes)), dma((GROUPS, lanes)),
        ],
        compiler_params=pltpu.CompilerParams(
            collective_id=0, has_side_effects=True, vmem_limit_bytes=56 * 2**20
        ),
        name="match",
    )(defocus_values, defocus_group, micrograph, templates, *held)
    return pl.pallas_call(
        functools.partial(finish, orients),
        out_shape=(jax.ShapeDtypeStruct((share, TS), f32),) * 4,
        in_specs=[VMEM],
        out_specs=(VMEM,) * 4,
        name="finish",
    )(merged)


def solution(mesh):
    placed = (P("tile", None), P("orient", "tile", None), P(), P("tile"))
    return jax.shard_map(
        functools.partial(per_device, mesh.shape["tile"], mesh.shape["orient"]),
        mesh=mesh,
        in_specs=placed,
        out_specs=(P(("tile", "orient"), None),) * 4,
        check_vma=False,
    )
```

time: 70.4 us -> 42.5 us (0.60)
  Pallas kernels: 55.5 us -> 41 us
  local copies, waits for them, and re-layouts: 8.83 us -> 0 us
  other arithmetic: 3.36 us -> 0 us
    pallas_call x3 -> x2, Pallas kernels: 55.5 us -> 41 us  [the longest x1 39.2 us: per_device(): pl.pallas_call(functools.partial(body, n, orients), out_shape=jax.ShapeDt...]
    unnamed x14 -> x0, local copies, waits for them, and re-layouts: 7.87 us -> none
    another operation x2 -> x0, other arithmetic: 1.35 us -> none  [contrast_vectors(): along = jnp.stack([jnp.sin(chi_k) * sign, jnp.cos(chi_k) * sign], axis=1)]
    reduce_sum x1 -> x0, other arithmetic: 1.26 us -> none  [per_device(): jnp.sum(jnp.where(group_ids == defocus_group[0], defocus_values, 0.0))]
    broadcast_in_dim x1 -> x0, local copies, waits for them, and re-layouts: 0.96 us -> none  [contrast_vectors(): return (along, down[:, :, None])]
    mul x1 -> x0, other arithmetic: 0.73 us -> none  [contrast_vectors(): factor * (wave * cos_j - AMPLITUDE * sin_j)]
where the time goes in v2:
time: 42.5 us; the launch traced here: 42.3 us
  Pallas kernels  41 us (96%)
  between operations  1.29 us (3%)
    pallas_call x1, Pallas kernels, per_device(): pl.pallas_call(functools.partial(body, n, orients), out_shape=jax.ShapeDt...  39.2 us
    pallas_call x1, Pallas kernels, per_device(): pl.pallas_call(functools.partial(finish, orients), out_shape=(jax.ShapeDt...  1.84 us

profile of v2, /device:TPU:1, one launch (start us, length us, event | category | flops | bytes accessed | tf_op | source)
XLA Modules:
  0.0 42.3 jit_solution(14324123400712796395)
XLA Ops:
  1.3 39.2 %match.1.merged_ref = f32[4,64,512]{2,1,0:T(8,128)} custom-call(f32[4]{0:T(128)} %values_ref.1, s32[1]{0:T(128)S(6)} %copy.14.group_ref, f32[512,512]{1,0:T(8,128)} %image_ref.1, f32[1,64,256]{2,1,0:T(8,128)} %tmpl_ref.1, bf16[800,768]{1,0:T(8,128)(2,1)} %constant.12.clone.rest_0_, bf16[800,768]{1,0:T(8,128)(2,1)} %constant.13.clone.rest_1_, ...), custom_call_target="tpu_custom_call" | custom-call | tf_op jit(solution)/shard_map/match/pallas_call | solution.py:291
  40.4 1.8 %finish.1 = (f32[64,512]{1,0:T(8,128)}, f32[64,512]{1,0:T(8,128)}, f32[64,512]{1,0:T(8,128)}, f32[64,512]{1,0:T(8,128)}) custom-call(f32[4,64,512]{2,1,0:T(8,128)} %match.1.merged_ref), custom_call_target="tpu_custom_call" | custom-call | tf_op jit(solution)/shard_map/finish/pallas_call | solution.py:323

commit v3 on v2

--- a/solution.py
+++ b/solution.py
@@ -63,7 +63,9 @@
 
 
 def dot3(a, b, contract=0):
-    return dot(a[0], b[0], contract) + (dot(a[0], b[1], contract) + dot(a[1], b[0], contract))
+    left = jnp.concatenate([a[0], a[1], a[0]], axis=1)
+    right = jnp.concatenate([b[0], b[0], b[1]], axis=contract)
+    return dot(left, right, contract)
 
 
 def circular(turns):

time: 42.5 us -> 42.4 us (level)
  no operation moved by 1% of the time
where the time goes in v3:
time: 42.4 us; the launch traced here: 42.2 us
  Pallas kernels  40.9 us (96%)
  between operations  1.29 us (3%)
    pallas_call x1, Pallas kernels, per_device(): pl.pallas_call(functools.partial(body, n, orients), out_shape=jax.ShapeDt...  39 us
    pallas_call x1, Pallas kernels, per_device(): pl.pallas_call(functools.partial(finish, orients), out_shape=(jax.ShapeDt...  1.84 us

profile of v3, /device:TPU:1, one launch (start us, length us, event | category | flops | bytes accessed | tf_op | source)
XLA Modules:
  0.0 42.2 jit_solution(6237711462909017246)
XLA Ops:
  1.3 39.0 %match.1.merged_ref = f32[4,64,512]{2,1,0:T(8,128)} custom-call(f32[4]{0:T(128)} %values_ref.1, s32[1]{0:T(128)S(6)} %copy.14.group_ref, f32[512,512]{1,0:T(8,128)} %image_ref.1, f32[1,64,256]{2,1,0:T(8,128)} %tmpl_ref.1, bf16[800,768]{1,0:T(8,128)(2,1)} %constant.12.clone.rest_0_, bf16[800,768]{1,0:T(8,128)(2,1)} %constant.13.clone.rest_1_, ...), custom_call_target="tpu_custom_call" | custom-call | tf_op jit(solution)/shard_map/match/pallas_call | solution.py:293
  40.3 1.8 %finish.1 = (f32[64,512]{1,0:T(8,128)}, f32[64,512]{1,0:T(8,128)}, f32[64,512]{1,0:T(8,128)}, f32[64,512]{1,0:T(8,128)}) custom-call(f32[4,64,512]{2,1,0:T(8,128)} %match.1.merged_ref), custom_call_target="tpu_custom_call" | custom-call | tf_op jit(solution)/shard_map/finish/pallas_call | solution.py:325

commit v4 on v3

--- a/solution.py
+++ b/solution.py
@@ -20,6 +20,8 @@
 WAVELENGTH = 0.0197
 AMPLITUDE = 0.07
 ROOT = math.sqrt(3.0) / 2.0
+RADIX = 6
+SUB = EXT // RADIX
 MESH = pl.DeviceIdType.MESH
 VMEM = pl.BlockSpec(memory_space=pltpu.VMEM)
 
@@ -36,10 +38,11 @@
     angle = 2.0 * np.pi * (j * n % EXT) / EXT
     rows = np.zeros((2 * FREQS, EXT))
     rows[: HALF + 1], rows[FREQS : FREQS + HALF + 1] = np.cos(angle), -np.sin(angle)
-    sample, a = np.arange(TPL)[:, None], np.arange(TPL)[None, :]
+    own = np.repeat(rows[:, MARGIN : MARGIN + TS].sum(axis=1, keepdims=True), 128, axis=1)
+    sample, a = np.arange(SUB)[:, None], np.arange(SUB)[None, :]
     cols = []
-    for b in range(3):
-        angle = 2.0 * np.pi * (sample * (3 * a + b) % EXT) / EXT
+    for b in range(RADIX):
+        angle = 2.0 * np.pi * (sample * (RADIX * a + b) % EXT) / EXT
         re, im = np.cos(angle), -np.sin(angle)
         cols.append(np.block([[re, im], [-im, re]]))
     p, j = np.arange(TS)[:, None], np.arange(HALF)[None, :]
@@ -48,7 +51,7 @@
     back_re[:, 0] = 1.0
     back_im[:, 0] = (-1.0) ** np.arange(TS)
     back = np.concatenate([back_re, back_im], axis=1)
-    return split_table(rows) + split_table(np.stack(cols)) + split_table(back)
+    return split_table(rows) + split_table(np.stack(cols)) + split_table(back) + (own.astype(np.float32),)
 
 
 def split(value):
@@ -66,6 +69,26 @@
     left = jnp.concatenate([a[0], a[1], a[0]], axis=1)
     right = jnp.concatenate([b[0], b[0], b[1]], axis=contract)
     return dot(left, right, contract)
+
+
+def turned(x, way):
+    re, im = x
+    return (way * ROOT) * im - 0.5 * re, (-way * ROOT) * re - 0.5 * im
+
+
+def plus(x, y):
+    return x[0] + y[0], x[1] + y[1]
+
+
+def minus(x, y):
+    return x[0] - y[0], x[1] - y[1]
+
+
+def three(x, y, z):
+    total, apart = plus(y, z), minus(y, z)
+    middle = x[0] - 0.5 * total[0], x[1] - 0.5 * total[1]
+    side = ROOT * apart[1], -ROOT * apart[0]
+    return plus(x, total), plus(middle, side), minus(middle, side)
 
 
 def circular(turns):
@@ -82,27 +105,26 @@
 
 
 def contrast_vectors(defocus):
-    a = lax.broadcasted_iota(jnp.int32, (8, TPL), 1)
-    b = lax.broadcasted_iota(jnp.int32, (8, TPL), 0)
-    k = 3 * a + b
+    a = lax.broadcasted_iota(jnp.int32, (8, SUB), 1)
+    b = lax.broadcasted_iota(jnp.int32, (8, SUB), 0)
+    k = RADIX * a + b
     k = jnp.where(k < HALF, k, k - EXT).astype(jnp.float32) * (1.0 / EXT)
     j = jnp.minimum(lax.broadcasted_iota(jnp.int32, (FREQS, 128), 0), HALF)
     j = j.astype(jnp.float32) * (1.0 / EXT)
-    sign = (1 - 2 * (a & 1)).astype(jnp.float32)
     rate = (WAVELENGTH / 2.0) * defocus
     sin_k, cos_k = circular(rate * (k * k))
     sin_j, cos_j = circular(rate * (j * j))
     wave = math.sqrt(1.0 - AMPLITUDE * AMPLITUDE)
     factor = -1.0 / (EXT * EXT)
     return (
-        (sin_k * sign, cos_k * sign),
+        (sin_k, cos_k),
         (factor * (wave * cos_j - AMPLITUDE * sin_j), factor * (wave * sin_j + AMPLITUDE * cos_j)),
     )
 
 
 def body(n, orients, values_ref, group_ref, image_ref, tmpl_ref, *rest):
-    hbm_tables, rest = rest[:6], rest[6:]
-    (out_ref, rows_h, rows_l, cols_h, cols_l, back_h, back_l, stats, halo, gath, win_h, win_l,
+    hbm_tables, rest = rest[:7], rest[7:]
+    (out_ref, rows_h, rows_l, cols_h, cols_l, back_h, back_l, own_sum, stats, halo, gath,
      along, down, half_spec, u_h, u_l, wide, v_h, v_l, backs, scores, landed,
      table_sem, stat_send, stat_recv, halo_send, halo_recv, far_send, far_recv,
      near_send, near_recv, pass_send, pass_recv, score_send, score_recv) = rest
@@ -135,7 +157,7 @@
     for step in range(1, lanes):
         pl.semaphore_signal(barrier, inc=1, device_id=lane(step), device_id_type=MESH)
 
-    held = (rows_h, rows_l, cols_h, cols_l, back_h, back_l)
+    held = (rows_h, rows_l, cols_h, cols_l, back_h, back_l, own_sum)
     loads = [pltpu.make_async_copy(src, dst, table_sem.at[i])
              for i, (src, dst) in enumerate(zip(hbm_tables, held))]
     for load in loads:
@@ -166,7 +188,12 @@
     wave_along, wave_down = contrast_vectors(values_ref[group_ref[0]])
     for i in range(2):
         along[i] = wave_along[i]
-        down[i] = wave_down[i]
+
+    local = jnp.full((1, TS), total, jnp.float32) * (1.0 / (TS * TS))
+    loads[0].wait()
+    loads[1].wait()
+    inner = slice(MARGIN, MARGIN + TS)
+    half_spec[...] = dot3((rows_h[:, inner], rows_l[:, inner]), split(image_ref[...] - local))
 
     for copy in stat_copies:
         copy.wait()
@@ -178,13 +205,12 @@
     square = jnp.sum(jnp.where(spot == 1, sums, 0.0)) / (8.0 * pixels)
     centre = jnp.full((1, TS), centre, jnp.float32)
     inverse = lax.rsqrt(square - centre * centre + 1e-05)
-    inner = pl.ds(MARGIN, TS)
-    win_h[inner], win_l[inner] = split((image_ref[...] - centre) * inverse)
+    for i in range(2):
+        down[i] = wave_down[i] * inverse[:, :128]
     for copy in halo_copies:
         copy.wait()
-    for i, (there, where) in enumerate(((me > 0, 0), (me < n - 1, MARGIN + TS))):
-        edge = jnp.where(there, (halo[i] - centre) * inverse, 0.0)
-        win_h[pl.ds(where, MARGIN)], win_l[pl.ds(where, MARGIN)] = split(edge)
+    before = jnp.where(me > 0, halo[0] - centre, 0.0)
+    after = jnp.where(me < n - 1, halo[1] - centre, 0.0)
 
     far_copy.wait()
     far_shard = gath.at[1 - mine, own_shard]
@@ -192,27 +218,29 @@
         send(far_shard, far_shard, pass_send.at[s], pass_recv.at[s], tile(s)) for s in range(1, n)
     ]
 
-    for load in loads:
+    edges = [jnp.concatenate([t[:, :MARGIN], t[:, MARGIN + TS :]], axis=1) for t in (rows_h, rows_l)]
+    edge_spec = dot3(edges, split(jnp.concatenate([before, after], axis=0)))
+    for load in loads[2:]:
         load.wait()
-    half_spec[...] = dot3((rows_h[...], rows_l[...]), (win_h[...], win_l[...]))
-    re0, re1 = half_spec[:FREQS, :TPL], half_spec[:FREQS, TPL:]
-    im0, im1 = half_spec[FREQS:, :TPL], half_spec[FREQS:, TPL:]
-    joined = (
-        (re0 + re1, im0 + im1),
-        (0.5 * re0 + ROOT * im0 - re1, 0.5 * im0 - ROOT * re0 - im1),
-        (re1 - 0.5 * re0 + ROOT * im0, im1 - 0.5 * im0 - ROOT * re0),
-    )
-    for b, (re, im) in enumerate(joined):
-        u_h[b, :, :TPL], u_l[b, :, :TPL] = split(re)
-        u_h[b, :, TPL:], u_l[b, :, TPL:] = split(im)
-
-    for b in range(3):
+    shift = own_sum[...] * (local - centre)[:, :128]
+    block = []
+    for m in range(TS // SUB):
+        here = slice(m * SUB, (m + 1) * SUB)
+        full = half_spec[:, here] + edge_spec[:, here] + shift
+        block.append((full[:FREQS], full[FREQS:]))
+    even = three(block[2], plus(block[0], block[3]), block[1])
+    flip = (-block[1][0], -block[1][1])
+    odd = three(block[2], minus(block[0], block[3]), flip)
+    odd = [(-re, -im) for re, im in odd]
+    for b, part in enumerate((even[0], odd[2], even[1], odd[0], even[2], odd[1])):
+        u_h[b, :, :SUB], u_l[b, :, :SUB] = split(part[0])
+        u_h[b, :, SUB:], u_l[b, :, SUB:] = split(part[1])
+
+    for b in range(RADIX):
         spec = dot3((u_h[b], u_l[b]), (cols_h[b], cols_l[b]))
-        for at in range(0, TPL, 128):
-            here = slice(at, at + 128)
-            contrast = along[0, b : b + 1, here] * down[0] + along[1, b : b + 1, here] * down[1]
-            wide[b, :, at : at + 128] = spec[:, at : at + 128] * contrast
-            wide[b, :, TPL + at : TPL + at + 128] = spec[:, TPL + at : TPL + at + 128] * contrast
+        contrast = along[0, b : b + 1] * down[0] + along[1, b : b + 1] * down[1]
+        wide[b, :, :SUB] = spec[:, :SUB] * contrast
+        wide[b, :, SUB:] = spec[:, SUB:] * contrast
 
     score_copies = []
     for turn in range(GROUPS):
@@ -223,26 +251,28 @@
         mean_square = jnp.full((1, TPL), jnp.sum(centred * centred) / (TPL * TPL), jnp.float32)
         normed = centred * (lax.rsqrt(mean_square + 1e-06) * (1.0 / TPL))
         first = dot3((rows_h[:, :TPL], rows_l[:, :TPL]), split(normed))
-        v_h[:, :TPL], v_l[:, :TPL] = split(first[:FREQS])
-        v_h[:, TPL:], v_l[:, TPL:] = split(first[FREQS:])
-
-        def branch(b, carry):
-            spec = dot3((v_h[...], v_l[...]), (cols_h[b], cols_l[b]))
-            w_re, w_im = wide[b, :, :TPL], wide[b, :, TPL:]
-            t_re, t_im = spec[:, :TPL], spec[:, TPL:]
+        near = first[:FREQS, :SUB], first[FREQS:, :SUB]
+        far = first[:FREQS, SUB:], first[FREQS:, SUB:]
+        once, twice = turned(far, 1), turned(far, -1)
+        parts = (plus(near, far), minus(near, twice), plus(near, once),
+                 minus(near, far), plus(near, twice), minus(near, once))
+        for b, (re, im) in enumerate(parts):
+            v_h[b, :, :SUB], v_l[b, :, :SUB] = split(re)
+            v_h[b, :, SUB:], v_l[b, :, SUB:] = split(im)
+
+        for b in range(RADIX):
+            spec = dot3((v_h[b], v_l[b]), (cols_h[b], cols_l[b]))
+            w_re, w_im = wide[b, :, :SUB], wide[b, :, SUB:]
+            t_re, t_im = spec[:, :SUB], spec[:, SUB:]
             prod = jnp.concatenate([w_re * t_re + w_im * t_im, w_im * t_re - w_re * t_im], axis=1)
             backs[b] = dot3(split(prod), (cols_h[b], cols_l[b]), 1)
-            return carry
-
-        lax.fori_loop(0, 3, branch, 0)
-        e_re, e_im = [backs[b, :, :TPL] for b in range(3)], [backs[b, :, TPL:] for b in range(3)]
-        sum_re, sum_im = e_re[1] + e_re[2], e_im[1] + e_im[2]
-        out_re = jnp.concatenate(
-            [e_re[0] + sum_re, e_re[0] - 0.5 * sum_re - ROOT * (e_im[1] - e_im[2])], axis=1
-        )
-        out_im = jnp.concatenate(
-            [e_im[0] + sum_im, e_im[0] - 0.5 * sum_im + ROOT * (e_re[1] - e_re[2])], axis=1
-        )
+
+        e = [(backs[b, :, :SUB], backs[b, :, SUB:]) for b in range(RADIX)]
+        even = three(e[0], e[2], e[4])
+        odd = three(e[3], e[5], e[1])
+        outs = plus(even[0], odd[0]), minus(even[2], odd[2]), plus(even[1], odd[1]), minus(even[0], odd[0])
+        out_re = jnp.concatenate([re for re, _ in outs], axis=1)
+        out_im = jnp.concatenate([im for _, im in outs], axis=1)
         top = lax.broadcasted_iota(jnp.int32, (HALF, 1), 0) == 0
         out_im = jnp.where(top, out_re[HALF : HALF + 1], out_im[:HALF])
         packed = split(jnp.concatenate([out_re[:HALF], out_im], axis=0))
@@ -293,26 +323,24 @@
     merged = pl.pallas_call(
         functools.partial(body, n, orients),
         out_shape=jax.ShapeDtypeStruct((4, share, TS), f32),
-        in_specs=[smem, smem, VMEM, VMEM] + [anywhere] * 6,
+        in_specs=[smem, smem, VMEM, VMEM] + [anywhere] * 7,
         out_specs=VMEM,
-        scratch_shapes=[vmem(t.shape, b16) for t in held] + [
+        scratch_shapes=[vmem(t.shape, t.dtype) for t in held] + [
             vmem((n, 8, 128), f32),
             vmem((2, MARGIN, TS), f32),
             vmem((GROUPS, TPL, TPL), f32),
-            vmem((EXT, TS), b16),
-            vmem((EXT, TS), b16),
-            vmem((2, 8, TPL), f32),
+            vmem((2, 8, SUB), f32),
             vmem((2, FREQS, 128), f32),
             vmem((2 * FREQS, TS), f32),
-            vmem((3, FREQS, TS), b16),
-            vmem((3, FREQS, TS), b16),
-            vmem((3, FREQS, TS), f32),
-            vmem((FREQS, TS), b16),
-            vmem((FREQS, TS), b16),
-            vmem((3, FREQS, TS), f32),
+            vmem((RADIX, FREQS, 2 * SUB), b16),
+            vmem((RADIX, FREQS, 2 * SUB), b16),
+            vmem((RADIX, FREQS, 2 * SUB), f32),
+            vmem((RADIX, FREQS, 2 * SUB), b16),
+            vmem((RADIX, FREQS, 2 * SUB), b16),
+            vmem((RADIX, FREQS, 2 * SUB), f32),
             vmem((GROUPS, TS // GROUPS, TS), f32),
             vmem((GROUPS, lanes, share, TS), f32),
-            dma((6,)),
+            dma((7,)),
             dma((n,)), dma((n,)), dma((2,)), dma((2,)), dma, dma,
             dma((n,)), dma((n,)), dma((n,)), dma((n,)),
             dma((GROUPS, lanes)), dma((GROUPS, lanes)),

time: 42.4 us -> 38.3 us (0.903)
  Pallas kernels: 40.9 us -> 36.8 us
    pallas_call x1, Pallas kernels: 39 us -> 35 us  [per_device(): pl.pallas_call(functools.partial(body, n, orients), out_shape=jax.ShapeDt...]
where the time goes in v4:
time: 38.3 us; the launch traced here: 38.1 us
  Pallas kernels  36.8 us (96%)
  between operations  1.29 us (3%)
    pallas_call x1, Pallas kernels, per_device(): pl.pallas_call(functools.partial(body, n, orients), out_shape=jax.ShapeDt...  35 us
    pallas_call x1, Pallas kernels, per_device(): pl.pallas_call(functools.partial(finish, orients), out_shape=(jax.ShapeDt...  1.84 us

profile of v4, /device:TPU:1, one launch (start us, length us, event | category | flops | bytes accessed | tf_op | source)
XLA Modules:
  0.0 38.1 jit_solution(1606537918030574346)
XLA Ops:
  1.3 35.0 %match.1.merged_ref = f32[4,64,512]{2,1,0:T(8,128)} custom-call(f32[4]{0:T(128)} %values_ref.1, s32[1]{0:T(128)S(6)} %copy.15.group_ref, f32[512,512]{1,0:T(8,128)} %image_ref.1, f32[1,64,256]{2,1,0:T(8,128)} %tmpl_ref.1, bf16[800,768]{1,0:T(8,128)(2,1)} %constant.14.clone.rest_0_, bf16[800,768]{1,0:T(8,128)(2,1)} %constant.15.clone.rest_1_, ...), custom_call_target="tpu_custom_call" | custom-call | tf_op jit(solution)/shard_map/match/pallas_call | solution.py:323
  36.3 1.8 %finish.1 = (f32[64,512]{1,0:T(8,128)}, f32[64,512]{1,0:T(8,128)}, f32[64,512]{1,0:T(8,128)}, f32[64,512]{1,0:T(8,128)}) custom-call(f32[4,64,512]{2,1,0:T(8,128)} %match.1.merged_ref), custom_call_target="tpu_custom_call" | custom-call | tf_op jit(solution)/shard_map/finish/pallas_call | solution.py:353

commit v5 on v4

--- a/solution.py
+++ b/solution.py
@@ -51,7 +51,10 @@
     back_re[:, 0] = 1.0
     back_im[:, 0] = (-1.0) ** np.arange(TS)
     back = np.concatenate([back_re, back_im], axis=1)
-    return split_table(rows) + split_table(np.stack(cols)) + split_table(back) + (own.astype(np.float32),)
+    cols = np.stack(cols)
+    inverse = np.swapaxes(cols, 1, 2)
+    return (split_table(rows) + split_table(cols) + (own.astype(np.float32),)
+            + split_table(inverse) + split_table(back))
 
 
 def split(value):
@@ -59,16 +62,10 @@
     return high, (value - high.astype(jnp.float32)).astype(jnp.bfloat16)
 
 
-def dot(a, b, contract=0):
-    return lax.dot_general(
-        a, b, (((1,), (contract,)), ((), ())), preferred_element_type=jnp.float32
-    )
-
-
-def dot3(a, b, contract=0):
+def dot3(a, b):
     left = jnp.concatenate([a[0], a[1], a[0]], axis=1)
-    right = jnp.concatenate([b[0], b[0], b[1]], axis=contract)
-    return dot(left, right, contract)
+    right = jnp.concatenate([b[0], b[0], b[1]], axis=0)
+    return jnp.dot(left, right, preferred_element_type=jnp.float32)
 
 
 def turned(x, way):
@@ -122,11 +119,11 @@
     )
 
 
-def body(n, orients, values_ref, group_ref, image_ref, tmpl_ref, *rest):
-    hbm_tables, rest = rest[:7], rest[7:]
-    (out_ref, rows_h, rows_l, cols_h, cols_l, back_h, back_l, own_sum, stats, halo, gath,
+def body(n, orients, values_ref, group_ref, image_hbm, tmpl_hbm, *rest):
+    hbm_tables, rest = rest[:9], rest[9:]
+    (out_ref, rows_h, rows_l, cols_h, cols_l, own_sum, inv_h, inv_l, back_h, back_l, image_ref, stats, halo, gath,
      along, down, half_spec, u_h, u_l, wide, v_h, v_l, backs, scores, landed,
-     table_sem, stat_send, stat_recv, halo_send, halo_recv, far_send, far_recv,
+     input_sem, table_sem, stat_send, stat_recv, halo_send, halo_recv, far_send, far_recv,
      near_send, near_recv, pass_send, pass_recv, score_send, score_recv) = rest
     me, orient = lax.axis_index("tile"), lax.axis_index("orient")
     lanes, share, shard = orients // GROUPS, TS // orients, TPL // n
@@ -157,34 +154,38 @@
     for step in range(1, lanes):
         pl.semaphore_signal(barrier, inc=1, device_id=lane(step), device_id_type=MESH)
 
-    held = (rows_h, rows_l, cols_h, cols_l, back_h, back_l, own_sum)
+    held = (rows_h, rows_l, cols_h, cols_l, own_sum, inv_h, inv_l, back_h, back_l)
     loads = [pltpu.make_async_copy(src, dst, table_sem.at[i])
              for i, (src, dst) in enumerate(zip(hbm_tables, held))]
-    for load in loads:
+    inputs = [
+        pltpu.make_async_copy(image_hbm, image_ref, input_sem.at[0]),
+        pltpu.make_async_copy(tmpl_hbm.at[0], gath.at[mine, own_shard], input_sem.at[1]),
+    ]
+    for load in inputs + loads:
         load.start()
+    for load in inputs:
+        load.wait()
 
     image = image_ref[...]
     total = jnp.sum(image)
     squares = jnp.sum(image * image)
     spot = lax.broadcasted_iota(jnp.int32, (8, 128), 1)
     stats[me] = jnp.where(spot == 0, total, jnp.where(spot == 1, squares, 0.0))
-    gath[mine, own_shard] = tmpl_ref[0]
 
     pl.semaphore_wait(barrier, (n - 1) + 1 + (lanes - 1))
     stat_copies = [
         send(stats.at[me], stats.at[me], stat_send.at[s], stat_recv.at[s], tile(s))
         for s in range(1, n)
     ]
+    near_copies = [
+        send(gath.at[mine, own_shard], gath.at[mine, own_shard], near_send.at[s], near_recv.at[s], tile(s))
+        for s in range(1, n)
+    ]
     halo_copies = [
         send(image_ref.at[pl.ds(TS - MARGIN, MARGIN)], halo.at[0], halo_send.at[0], halo_recv.at[0], tile(1)),
         send(image_ref.at[pl.ds(0, MARGIN)], halo.at[1], halo_send.at[1], halo_recv.at[1], tile(n - 1)),
     ]
-    far_copy = send(tmpl_ref.at[0], gath.at[mine, own_shard], far_send, far_recv, across)
-    near_copies = [
-        send(tmpl_ref.at[0], gath.at[mine, own_shard], near_send.at[s], near_recv.at[s], tile(s))
-        for s in range(1, n)
-    ]
-
+    far_copy = send(gath.at[mine, own_shard], gath.at[mine, own_shard], far_send, far_recv, across)
     wave_along, wave_down = contrast_vectors(values_ref[group_ref[0]])
     for i in range(2):
         along[i] = wave_along[i]
@@ -194,6 +195,25 @@
     loads[1].wait()
     inner = slice(MARGIN, MARGIN + TS)
     half_spec[...] = dot3((rows_h[:, inner], rows_l[:, inner]), split(image_ref[...] - local))
+
+    def forward(which):
+        tmpl = gath[which]
+        centred = tmpl - jnp.sum(tmpl) / (TPL * TPL)
+        mean_square = jnp.full((1, TPL), jnp.sum(centred * centred) / (TPL * TPL), jnp.float32)
+        normed = centred * (lax.rsqrt(mean_square + 1e-06) * (1.0 / TPL))
+        first = dot3((rows_h[:, :TPL], rows_l[:, :TPL]), split(normed))
+        near = first[:FREQS, :SUB], first[FREQS:, :SUB]
+        far = first[:FREQS, SUB:], first[FREQS:, SUB:]
+        once, twice = turned(far, 1), turned(far, -1)
+        parts = (plus(near, far), minus(near, twice), plus(near, once),
+                 minus(near, far), plus(near, twice), minus(near, once))
+        for b, (re, im) in enumerate(parts):
+            v_h[b, :, :SUB], v_l[b, :, :SUB] = split(re)
+            v_h[b, :, SUB:], v_l[b, :, SUB:] = split(im)
+
+    for copy in near_copies:
+        copy.wait()
+    forward(mine)
 
     for copy in stat_copies:
         copy.wait()
@@ -244,28 +264,16 @@
 
     score_copies = []
     for turn in range(GROUPS):
-        for copy in near_copies if turn == 0 else pass_copies:
-            copy.wait()
-        tmpl = gath[mine if turn == 0 else 1 - mine]
-        centred = tmpl - jnp.sum(tmpl) / (TPL * TPL)
-        mean_square = jnp.full((1, TPL), jnp.sum(centred * centred) / (TPL * TPL), jnp.float32)
-        normed = centred * (lax.rsqrt(mean_square + 1e-06) * (1.0 / TPL))
-        first = dot3((rows_h[:, :TPL], rows_l[:, :TPL]), split(normed))
-        near = first[:FREQS, :SUB], first[FREQS:, :SUB]
-        far = first[:FREQS, SUB:], first[FREQS:, SUB:]
-        once, twice = turned(far, 1), turned(far, -1)
-        parts = (plus(near, far), minus(near, twice), plus(near, once),
-                 minus(near, far), plus(near, twice), minus(near, once))
-        for b, (re, im) in enumerate(parts):
-            v_h[b, :, :SUB], v_l[b, :, :SUB] = split(re)
-            v_h[b, :, SUB:], v_l[b, :, SUB:] = split(im)
-
+        if turn:
+            for copy in pass_copies:
+                copy.wait()
+            forward(1 - mine)
         for b in range(RADIX):
             spec = dot3((v_h[b], v_l[b]), (cols_h[b], cols_l[b]))
             w_re, w_im = wide[b, :, :SUB], wide[b, :, SUB:]
             t_re, t_im = spec[:, :SUB], spec[:, SUB:]
             prod = jnp.concatenate([w_re * t_re + w_im * t_im, w_im * t_re - w_re * t_im], axis=1)
-            backs[b] = dot3(split(prod), (cols_h[b], cols_l[b]), 1)
+            backs[b] = dot3(split(prod), (inv_h[b], inv_l[b]))
 
         e = [(backs[b, :, :SUB], backs[b, :, SUB:]) for b in range(RADIX)]
         even = three(e[0], e[2], e[4])
@@ -290,10 +298,9 @@
     first, other = scores[0, own], scores[1, own]
     best, second = jnp.maximum(first, other), jnp.minimum(first, other)
     total, squares = first + other, first * first + other * other
-    for copy in score_copies:
-        copy.wait()
     for g in range(GROUPS):
         for step in range(1, lanes):
+            score_copies[g * (lanes - 1) + step - 1].wait()
             score = landed[g, step]
             second = jnp.maximum(second, jnp.minimum(best, score))
             best = jnp.maximum(best, score)
@@ -323,9 +330,10 @@
     merged = pl.pallas_call(
         functools.partial(body, n, orients),
         out_shape=jax.ShapeDtypeStruct((4, share, TS), f32),
-        in_specs=[smem, smem, VMEM, VMEM] + [anywhere] * 7,
+        in_specs=[smem, smem] + [anywhere] * 11,
         out_specs=VMEM,
         scratch_shapes=[vmem(t.shape, t.dtype) for t in held] + [
+            vmem((TS, TS), f32),
             vmem((n, 8, 128), f32),
             vmem((2, MARGIN, TS), f32),
             vmem((GROUPS, TPL, TPL), f32),
@@ -340,7 +348,7 @@
             vmem((RADIX, FREQS, 2 * SUB), f32),
             vmem((GROUPS, TS // GROUPS, TS), f32),
             vmem((GROUPS, lanes, share, TS), f32),
-            dma((7,)),
+            dma((2,)), dma((9,)),
             dma((n,)), dma((n,)), dma((2,)), dma((2,)), dma, dma,
             dma((n,)), dma((n,)), dma((n,)), dma((n,)),
             dma((GROUPS, lanes)), dma((GROUPS, lanes)),

time: 38.3 us -> 40.2 us (1.050)
  Pallas kernels: 36.8 us -> 38.4 us
    pallas_call x1, Pallas kernels: 35 us -> 36.6 us  [per_device(): pl.pallas_call(functools.partial(body, n, orients), out_shape=jax.ShapeDt...]
where the time goes in v5:
time: 40.2 us; the launch traced here: 39.7 us
  Pallas kernels  38.4 us (96%)
  between operations  1.29 us (3%)
    pallas_call x1, Pallas kernels, per_device(): pl.pallas_call(functools.partial(body, n, orients), out_shape=jax.ShapeDt...  36.6 us
    pallas_call x1, Pallas kernels, per_device(): pl.pallas_call(functools.partial(finish, orients), out_shape=(jax.ShapeDt...  1.84 us

profile of v5, /device:TPU:1, one launch (start us, length us, event | category | flops | bytes accessed | tf_op | source)
XLA Modules:
  0.0 39.7 jit_solution(16725254782939142193)
XLA Ops:
  1.3 36.6 %match.1.merged_ref = f32[4,64,512]{2,1,0:T(8,128)} custom-call(f32[4]{0:T(128)} %values_ref.1, s32[1]{0:T(128)S(6)} %copy.17.group_ref, f32[512,512]{1,0:T(8,128)} %image_hbm.1, f32[1,64,256]{2,1,0:T(8,128)} %tmpl_hbm.1, bf16[800,768]{1,0:T(8,128)(2,1)} %constant.18.clone.rest_0_, bf16[800,768]{1,0:T(8,128)(2,1)} %constant.19.clone.rest_1_, ...), custom_call_target="tpu_custom_call" | custom-call | tf_op jit(solution)/shard_map/match/pallas_call | solution.py:330
  37.8 1.8 %finish.1 = (f32[64,512]{1,0:T(8,128)}, f32[64,512]{1,0:T(8,128)}, f32[64,512]{1,0:T(8,128)}, f32[64,512]{1,0:T(8,128)}) custom-call(f32[4,64,512]{2,1,0:T(8,128)} %match.1.merged_ref), custom_call_target="tpu_custom_call" | custom-call | tf_op jit(solution)/shard_map/finish/pallas_call | solution.py:361

commit v6 on v4

--- a/solution.py
+++ b/solution.py
@@ -122,11 +122,11 @@
     )
 
 
-def body(n, orients, values_ref, group_ref, image_ref, tmpl_ref, *rest):
+def body(n, orients, values_ref, group_ref, image_hbm, tmpl_hbm, *rest):
     hbm_tables, rest = rest[:7], rest[7:]
-    (out_ref, rows_h, rows_l, cols_h, cols_l, back_h, back_l, own_sum, stats, halo, gath,
+    (out_ref, rows_h, rows_l, cols_h, cols_l, back_h, back_l, own_sum, image_ref, stats, halo, gath,
      along, down, half_spec, u_h, u_l, wide, v_h, v_l, backs, scores, landed,
-     table_sem, stat_send, stat_recv, halo_send, halo_recv, far_send, far_recv,
+     input_sem, table_sem, stat_send, stat_recv, halo_send, halo_recv, far_send, far_recv,
      near_send, near_recv, pass_send, pass_recv, score_send, score_recv) = rest
     me, orient = lax.axis_index("tile"), lax.axis_index("orient")
     lanes, share, shard = orients // GROUPS, TS // orients, TPL // n
@@ -160,15 +160,20 @@
     held = (rows_h, rows_l, cols_h, cols_l, back_h, back_l, own_sum)
     loads = [pltpu.make_async_copy(src, dst, table_sem.at[i])
              for i, (src, dst) in enumerate(zip(hbm_tables, held))]
-    for load in loads:
+    inputs = [
+        pltpu.make_async_copy(image_hbm, image_ref, input_sem.at[0]),
+        pltpu.make_async_copy(tmpl_hbm.at[0], gath.at[mine, own_shard], input_sem.at[1]),
+    ]
+    for load in inputs + loads:
         load.start()
+    for load in inputs:
+        load.wait()
 
     image = image_ref[...]
     total = jnp.sum(image)
     squares = jnp.sum(image * image)
     spot = lax.broadcasted_iota(jnp.int32, (8, 128), 1)
     stats[me] = jnp.where(spot == 0, total, jnp.where(spot == 1, squares, 0.0))
-    gath[mine, own_shard] = tmpl_ref[0]
 
     pl.semaphore_wait(barrier, (n - 1) + 1 + (lanes - 1))
     stat_copies = [
@@ -179,9 +184,9 @@
         send(image_ref.at[pl.ds(TS - MARGIN, MARGIN)], halo.at[0], halo_send.at[0], halo_recv.at[0], tile(1)),
         send(image_ref.at[pl.ds(0, MARGIN)], halo.at[1], halo_send.at[1], halo_recv.at[1], tile(n - 1)),
     ]
-    far_copy = send(tmpl_ref.at[0], gath.at[mine, own_shard], far_send, far_recv, across)
+    far_copy = send(gath.at[mine, own_shard], gath.at[mine, own_shard], far_send, far_recv, across)
     near_copies = [
-        send(tmpl_ref.at[0], gath.at[mine, own_shard], near_send.at[s], near_recv.at[s], tile(s))
+        send(gath.at[mine, own_shard], gath.at[mine, own_shard], near_send.at[s], near_recv.at[s], tile(s))
         for s in range(1, n)
     ]
 
@@ -236,17 +241,8 @@
         u_h[b, :, :SUB], u_l[b, :, :SUB] = split(part[0])
         u_h[b, :, SUB:], u_l[b, :, SUB:] = split(part[1])
 
-    for b in range(RADIX):
-        spec = dot3((u_h[b], u_l[b]), (cols_h[b], cols_l[b]))
-        contrast = along[0, b : b + 1] * down[0] + along[1, b : b + 1] * down[1]
-        wide[b, :, :SUB] = spec[:, :SUB] * contrast
-        wide[b, :, SUB:] = spec[:, SUB:] * contrast
-
-    score_copies = []
-    for turn in range(GROUPS):
-        for copy in near_copies if turn == 0 else pass_copies:
-            copy.wait()
-        tmpl = gath[mine if turn == 0 else 1 - mine]
+    def forward(which):
+        tmpl = gath[which]
         centred = tmpl - jnp.sum(tmpl) / (TPL * TPL)
         mean_square = jnp.full((1, TPL), jnp.sum(centred * centred) / (TPL * TPL), jnp.float32)
         normed = centred * (lax.rsqrt(mean_square + 1e-06) * (1.0 / TPL))
@@ -260,6 +256,21 @@
             v_h[b, :, :SUB], v_l[b, :, :SUB] = split(re)
             v_h[b, :, SUB:], v_l[b, :, SUB:] = split(im)
 
+    for copy in near_copies:
+        copy.wait()
+    forward(mine)
+    for b in range(RADIX):
+        spec = dot3((u_h[b], u_l[b]), (cols_h[b], cols_l[b]))
+        contrast = along[0, b : b + 1] * down[0] + along[1, b : b + 1] * down[1]
+        wide[b, :, :SUB] = spec[:, :SUB] * contrast
+        wide[b, :, SUB:] = spec[:, SUB:] * contrast
+
+    score_copies = []
+    for turn in range(GROUPS):
+        if turn:
+            for copy in pass_copies:
+                copy.wait()
+            forward(1 - mine)
         for b in range(RADIX):
             spec = dot3((v_h[b], v_l[b]), (cols_h[b], cols_l[b]))
             w_re, w_im = wide[b, :, :SUB], wide[b, :, SUB:]
@@ -290,10 +301,9 @@
     first, other = scores[0, own], scores[1, own]
     best, second = jnp.maximum(first, other), jnp.minimum(first, other)
     total, squares = first + other, first * first + other * other
-    for copy in score_copies:
-        copy.wait()
     for g in range(GROUPS):
         for step in range(1, lanes):
+            score_copies[g * (lanes - 1) + step - 1].wait()
             score = landed[g, step]
             second = jnp.maximum(second, jnp.minimum(best, score))
             best = jnp.maximum(best, score)
@@ -301,16 +311,18 @@
             squares = squares + score * score
     out_ref[0] = best
     out_ref[1] = second
-    out_ref[2] = total
-    out_ref[3] = squares
-
-
-def finish(orients, merged_ref, best_ref, second_ref, mean_ref, var_ref):
-    best_ref[...] = merged_ref[0]
-    second_ref[...] = merged_ref[1]
-    mean = merged_ref[2] / orients
-    mean_ref[...] = mean
-    var_ref[...] = merged_ref[3] / orients - mean * mean
+    mean = total / orients
+    out_ref[2] = mean
+    out_ref[3] = squares / orients - mean * mean
+
+
+def finish(merged_ref, *rest):
+    outs, sems = rest[:4], rest[4]
+    copies = [pltpu.make_async_copy(merged_ref.at[i], out, sems.at[i]) for i, out in enumerate(outs)]
+    for copy in copies:
+        copy.start()
+    for copy in copies:
+        copy.wait()
 
 
 def per_device(n, orients, micrograph, templates, defocus_values, defocus_group):
@@ -323,9 +335,10 @@
     merged = pl.pallas_call(
         functools.partial(body, n, orients),
         out_shape=jax.ShapeDtypeStruct((4, share, TS), f32),
-        in_specs=[smem, smem, VMEM, VMEM] + [anywhere] * 7,
+        in_specs=[smem, smem] + [anywhere] * 9,
         out_specs=VMEM,
         scratch_shapes=[vmem(t.shape, t.dtype) for t in held] + [
+            vmem((TS, TS), f32),
             vmem((n, 8, 128), f32),
             vmem((2, MARGIN, TS), f32),
             vmem((GROUPS, TPL, TPL), f32),
@@ -340,7 +353,7 @@
             vmem((RADIX, FREQS, 2 * SUB), f32),
             vmem((GROUPS, TS // GROUPS, TS), f32),
             vmem((GROUPS, lanes, share, TS), f32),
-            dma((7,)),
+            dma((2,)), dma((7,)),
             dma((n,)), dma((n,)), dma((2,)), dma((2,)), dma, dma,
             dma((n,)), dma((n,)), dma((n,)), dma((n,)),
             dma((GROUPS, lanes)), dma((GROUPS, lanes)),
@@ -351,10 +364,11 @@
         name="match",
     )(defocus_values, defocus_group, micrograph, templates, *held)
     return pl.pallas_call(
-        functools.partial(finish, orients),
+        finish,
         out_shape=(jax.ShapeDtypeStruct((share, TS), f32),) * 4,
-        in_specs=[VMEM],
-        out_specs=(VMEM,) * 4,
+        in_specs=[anywhere],
+        out_specs=(anywhere,) * 4,
+        scratch_shapes=[dma((4,))],
         name="finish",
     )(merged)
 

time: 38.3 us -> 54.3 us (1.42)
  Pallas kernels: 36.8 us -> 52.8 us
    pallas_call x1, Pallas kernels: 1.84 us -> 17 us  [per_device(): pl.pallas_call(finish, out_shape=(jax.ShapeDtypeStruct((share, TS), f32),...]
    pallas_call x1, Pallas kernels: 35 us -> 35.8 us  [per_device(): pl.pallas_call(functools.partial(body, n, orients), out_shape=jax.ShapeDt...]
where the time goes in v6:
time: 54.3 us; the launch traced here: 54.1 us
  Pallas kernels  52.8 us (97%)
  between operations  1.29 us (2%)
    pallas_call x1, Pallas kernels, per_device(): pl.pallas_call(functools.partial(body, n, orients), out_shape=jax.ShapeDt...  35.8 us
    pallas_call x1, Pallas kernels, per_device(): pl.pallas_call(finish, out_shape=(jax.ShapeDtypeStruct((share, TS), f32),...  17 us

profile of v6, /device:TPU:1, one launch (start us, length us, event | category | flops | bytes accessed | tf_op | source)
XLA Modules:
  0.0 54.1 jit_solution(13362482833143029569)
XLA Ops:
  1.3 35.8 %match.1.merged_ref = f32[4,64,512]{2,1,0:T(8,128)} custom-call(f32[4]{0:T(128)} %values_ref.1, s32[1]{0:T(128)S(6)} %copy.15.group_ref, f32[512,512]{1,0:T(8,128)} %image_hbm.1, f32[1,64,256]{2,1,0:T(8,128)} %tmpl_hbm.1, bf16[800,768]{1,0:T(8,128)(2,1)} %constant.14.clone.rest_0_, bf16[800,768]{1,0:T(8,128)(2,1)} %constant.15.clone.rest_1_, ...), custom_call_target="tpu_custom_call" | custom-call | tf_op jit(solution)/shard_map/match/pallas_call | solution.py:335
  37.1 17.0 %finish.1 = (f32[64,512]{1,0:T(8,128)}, f32[64,512]{1,0:T(8,128)}, f32[64,512]{1,0:T(8,128)}, f32[64,512]{1,0:T(8,128)}) custom-call(f32[4,64,512]{2,1,0:T(8,128)} %match.1.merged_ref), custom_call_target="tpu_custom_call" | custom-call | tf_op jit(solution)/shard_map/finish/pallas_call | solution.py:366

commit v7 on v6

--- a/solution.py
+++ b/solution.py
@@ -38,7 +38,10 @@
     angle = 2.0 * np.pi * (j * n % EXT) / EXT
     rows = np.zeros((2 * FREQS, EXT))
     rows[: HALF + 1], rows[FREQS : FREQS + HALF + 1] = np.cos(angle), -np.sin(angle)
-    own = np.repeat(rows[:, MARGIN : MARGIN + TS].sum(axis=1, keepdims=True), 128, axis=1)
+    own = np.stack([
+        np.repeat(rows[:, part].sum(axis=1, keepdims=True), 128, axis=1)
+        for part in (slice(MARGIN, MARGIN + TS), slice(0, MARGIN), slice(MARGIN + TS, EXT))
+    ])
     sample, a = np.arange(SUB)[:, None], np.arange(SUB)[None, :]
     cols = []
     for b in range(RADIX):
@@ -166,6 +169,11 @@
     ]
     for load in inputs + loads:
         load.start()
+    pl.semaphore_wait(barrier, (n - 1) + 1 + (lanes - 1))
+    halo_copies = [
+        send(image_hbm.at[pl.ds(TS - MARGIN, MARGIN)], halo.at[0], halo_send.at[0], halo_recv.at[0], tile(1)),
+        send(image_hbm.at[pl.ds(0, MARGIN)], halo.at[1], halo_send.at[1], halo_recv.at[1], tile(n - 1)),
+    ]
     for load in inputs:
         load.wait()
 
@@ -174,19 +182,13 @@
     squares = jnp.sum(image * image)
     spot = lax.broadcasted_iota(jnp.int32, (8, 128), 1)
     stats[me] = jnp.where(spot == 0, total, jnp.where(spot == 1, squares, 0.0))
-
-    pl.semaphore_wait(barrier, (n - 1) + 1 + (lanes - 1))
     stat_copies = [
         send(stats.at[me], stats.at[me], stat_send.at[s], stat_recv.at[s], tile(s))
         for s in range(1, n)
     ]
-    halo_copies = [
-        send(image_ref.at[pl.ds(TS - MARGIN, MARGIN)], halo.at[0], halo_send.at[0], halo_recv.at[0], tile(1)),
-        send(image_ref.at[pl.ds(0, MARGIN)], halo.at[1], halo_send.at[1], halo_recv.at[1], tile(n - 1)),
-    ]
-    far_copy = send(gath.at[mine, own_shard], gath.at[mine, own_shard], far_send, far_recv, across)
+    far_copy = send(tmpl_hbm.at[0], gath.at[mine, own_shard], far_send, far_recv, across)
     near_copies = [
-        send(gath.at[mine, own_shard], gath.at[mine, own_shard], near_send.at[s], near_recv.at[s], tile(s))
+        send(tmpl_hbm.at[0], gath.at[mine, own_shard], near_send.at[s], near_recv.at[s], tile(s))
         for s in range(1, n)
     ]
 
@@ -200,6 +202,13 @@
     inner = slice(MARGIN, MARGIN + TS)
     half_spec[...] = dot3((rows_h[:, inner], rows_l[:, inner]), split(image_ref[...] - local))
 
+    for copy in halo_copies:
+        copy.wait()
+    before = jnp.where(me > 0, halo[0] - local, 0.0)
+    after = jnp.where(me < n - 1, halo[1] - local, 0.0)
+
+    edges = [jnp.concatenate([t[:, :MARGIN], t[:, MARGIN + TS :]], axis=1) for t in (rows_h, rows_l)]
+    edge_spec = dot3(edges, split(jnp.concatenate([before, after], axis=0)))
     for copy in stat_copies:
         copy.wait()
     sums = stats[0]
@@ -212,22 +221,11 @@
     inverse = lax.rsqrt(square - centre * centre + 1e-05)
     for i in range(2):
         down[i] = wave_down[i] * inverse[:, :128]
-    for copy in halo_copies:
-        copy.wait()
-    before = jnp.where(me > 0, halo[0] - centre, 0.0)
-    after = jnp.where(me < n - 1, halo[1] - centre, 0.0)
-
-    far_copy.wait()
-    far_shard = gath.at[1 - mine, own_shard]
-    pass_copies = [
-        send(far_shard, far_shard, pass_send.at[s], pass_recv.at[s], tile(s)) for s in range(1, n)
-    ]
-
-    edges = [jnp.concatenate([t[:, :MARGIN], t[:, MARGIN + TS :]], axis=1) for t in (rows_h, rows_l)]
-    edge_spec = dot3(edges, split(jnp.concatenate([before, after], axis=0)))
     for load in loads[2:]:
         load.wait()
-    shift = own_sum[...] * (local - centre)[:, :128]
+    present = own_sum[0] + jnp.where(me > 0, own_sum[1], 0.0)
+    present = present + jnp.where(me < n - 1, own_sum[2], 0.0)
+    shift = present * (local - centre)[:, :128]
     block = []
     for m in range(TS // SUB):
         here = slice(m * SUB, (m + 1) * SUB)
@@ -256,9 +254,11 @@
             v_h[b, :, :SUB], v_l[b, :, :SUB] = split(re)
             v_h[b, :, SUB:], v_l[b, :, SUB:] = split(im)
 
-    for copy in near_copies:
-        copy.wait()
-    forward(mine)
+    far_copy.wait()
+    far_shard = gath.at[1 - mine, own_shard]
+    pass_copies = [
+        send(far_shard, far_shard, pass_send.at[s], pass_recv.at[s], tile(s)) for s in range(1, n)
+    ]
     for b in range(RADIX):
         spec = dot3((u_h[b], u_l[b]), (cols_h[b], cols_l[b]))
         contrast = along[0, b : b + 1] * down[0] + along[1, b : b + 1] * down[1]
@@ -267,10 +267,9 @@
 
     score_copies = []
     for turn in range(GROUPS):
-        if turn:
-            for copy in pass_copies:
-                copy.wait()
-            forward(1 - mine)
+        for copy in pass_copies if turn else near_copies:
+            copy.wait()
+        forward(1 - mine if turn else mine)
         for b in range(RADIX):
             spec = dot3((v_h[b], v_l[b]), (cols_h[b], cols_l[b]))
             w_re, w_im = wide[b, :, :SUB], wide[b, :, SUB:]
@@ -316,13 +315,9 @@
     out_ref[3] = squares / orients - mean * mean
 
 
-def finish(merged_ref, *rest):
-    outs, sems = rest[:4], rest[4]
-    copies = [pltpu.make_async_copy(merged_ref.at[i], out, sems.at[i]) for i, out in enumerate(outs)]
-    for copy in copies:
-        copy.start()
-    for copy in copies:
-        copy.wait()
+def finish(merged_ref, *outs):
+    for i, out in enumerate(outs):
+        out[...] = merged_ref[i]
 
 
 def per_device(n, orients, micrograph, templates, defocus_values, defocus_group):
@@ -366,9 +361,8 @@
     return pl.pallas_call(
         finish,
         out_shape=(jax.ShapeDtypeStruct((share, TS), f32),) * 4,
-        in_specs=[anywhere],
-        out_specs=(anywhere,) * 4,
-        scratch_shapes=[dma((4,))],
+        in_specs=[VMEM],
+        out_specs=(VMEM,) * 4,
         name="finish",
     )(merged)
 

time: 54.3 us -> 39.5 us (0.73)
  Pallas kernels: 52.8 us -> 37.5 us
    pallas_call x1, Pallas kernels: 17 us -> 1.84 us  [per_device(): pl.pallas_call(finish, out_shape=(jax.ShapeDtypeStruct((share, TS), f32),...]
where the time goes in v7:
time: 39.5 us; the launch traced here: 38.8 us
  Pallas kernels  37.5 us (95%)
  between operations  1.29 us (3%)
    pallas_call x1, Pallas kernels, per_device(): pl.pallas_call(functools.partial(body, n, orients), out_shape=jax.ShapeDt...  35.7 us
    pallas_call x1, Pallas kernels, per_device(): pl.pallas_call(finish, out_shape=(jax.ShapeDtypeStruct((share, TS), f32),...  1.84 us

profile of v7, /device:TPU:1, one launch (start us, length us, event | category | flops | bytes accessed | tf_op | source)
XLA Modules:
  0.0 38.8 jit_solution(1563351025324295441)
XLA Ops:
  1.3 35.7 %match.1.merged_ref = f32[4,64,512]{2,1,0:T(8,128)} custom-call(f32[4]{0:T(128)} %values_ref.1, s32[1]{0:T(128)S(6)} %copy.15.group_ref, f32[512,512]{1,0:T(8,128)} %image_hbm.1, f32[1,64,256]{2,1,0:T(8,128)} %tmpl_hbm.1, bf16[800,768]{1,0:T(8,128)(2,1)} %constant.14.clone.rest_0_, bf16[800,768]{1,0:T(8,128)(2,1)} %constant.15.clone.rest_1_, ...), custom_call_target="tpu_custom_call" | custom-call | tf_op jit(solution)/shard_map/match/pallas_call | solution.py:330
  37.0 1.8 %finish.1 = (f32[64,512]{1,0:T(8,128)}, f32[64,512]{1,0:T(8,128)}, f32[64,512]{1,0:T(8,128)}, f32[64,512]{1,0:T(8,128)}) custom-call(f32[4,64,512]{2,1,0:T(8,128)} %match.1.merged_ref), custom_call_target="tpu_custom_call" | custom-call | tf_op jit(solution)/shard_map/finish/pallas_call | solution.py:361
